TPU v7x, 512 devices: a whole 4x8x8 slice. The times are simulated.
512 devices in a mesh: row: 32 (over x, y), col: 16 (over z, core).
Axes of the slice: x: 4, y: 8, z: 8, core: 2. Of those that a mesh axis runs over, the one named last changes fastest.
Arguments:
- gate_pre: bfloat16 [2048, 28672], P('col', 'row'), may hold values from -6 to 6
- up_pre: bfloat16 [2048, 28672], P('col', 'row'), may hold values from -6 to 6
- down_weight: bfloat16 [28672, 4096], P('row', 'col'), may hold values from -0.03125 to 0.03125
- out_grad: bfloat16 [2048, 4096], P('col', 'row'), may hold values from -6 to 6
Outputs:
- output: bfloat16 [2048, 4096], P('col', 'row')
- gate_grad: bfloat16 [2048, 28672], P('col', 'row')
- up_grad: bfloat16 [2048, 28672], P('col', 'row')
- weight_grad: bfloat16 [28672, 4096], P('row', 'col')
All inputs are finite; a program needn't handle non-finite values.
Results may differ from a plain program's by a relative error of at most 0.0049.
Values may be sent and summed in bfloat16 or wider, within the bound.
No kernel may reach another device: no remote copies, remote signals or barrier semaphores. Data moves between devices by JAX's collectives and lax.ppermute only.
A program may use at most 64 MiB of HBM per device.

v0:
```python
import jax
import jax.numpy as jnp
from jax import lax
from jax.sharding import PartitionSpec as P


def body(gate_pre, up_pre, down_weight, out_grad):
    gate_value = gate_pre.astype(jnp.float32)
    up_value = up_pre.astype(jnp.float32)
    sigmoid_gate = jax.nn.sigmoid(gate_value)
    hidden = (gate_value * sigmoid_gate * up_value).astype(jnp.bfloat16)
    weights = lax.all_gather(down_weight, "col", axis=1, tiled=True)
    own_block = lax.psum_scatter(
        lax.dot_general(
            weights, hidden, (((0,), (1,)), ((), ())), preferred_element_type=jnp.float32
        ),
        "row",
        scatter_dimension=0,
        tiled=True,
    ).T
    output = own_block.astype(jnp.bfloat16)
    grad_full = lax.all_gather(out_grad, "row", axis=1, tiled=True)
    hidden_grad = lax.dot_general(
        grad_full, weights, (((1,), (1,)), ((), ())), preferred_element_type=jnp.float32
    )
    gate_grad = hidden_grad * up_value * sigmoid_gate * (1.0 + gate_value * (1.0 - sigmoid_gate))
    up_grad = hidden_grad * gate_value * sigmoid_gate
    grad_by_token = lax.all_to_all(grad_full, "col", split_axis=1, concat_axis=0, tiled=True)
    weight_grad = lax.dot_general(
        lax.all_gather(hidden, "col", axis=0, tiled=True),
        grad_by_token,
        (((0,), (0,)), ((), ())),
        preferred_element_type=jnp.float32,
    )
    return (
        output,
        gate_grad.astype(jnp.bfloat16),
        up_grad.astype(jnp.bfloat16),
        weight_grad.astype(jnp.bfloat16),
    )


def solution(mesh):
    placed = (P("col", "row"), P("col", "row"), P("row", "col"), P("col", "row"))
    return jax.shard_map(
        body,
        mesh=mesh,
        in_specs=placed,
        out_specs=(P("col", "row"), P("col", "row"), P("col", "row"), P("row", "col")),
        check_vma=False,
    )
```

profile of v0, /device:TPU:1, one launch (start us, length us, event | category | flops | bytes accessed | tf_op | source)
XLA Modules:
  0.0 452.3 jit_solution(1205828446620291213)
XLA Ops:
  7.2 0.0 all-gather.6.cloned.1.call-start
  7.2 1.5 copy.8
  8.7 0.0 all-gather.6.cloned.1.call-update
  8.7 0.0 all-gather.4.cloned.1.call-start
  8.8 0.7 all-gather.4.cloned.1.call-update
  9.5 0.0 reduce-scatter.2.cloned.1.call-start
  9.5 84.8 %all-gather.6.cloned.1.call-done = bf16[128,4096]{0,1:T(8,128)(2,1)} async-done(((bf16[128,128]{0,1:T(8,128)(2,1)}), bf16[128,4096]{0,1:T(8,128)(2,1)}) %all-gather.6.cloned.1.call-update) | async-done | bytes 1048592 | tf_op jit(solution)/shard_map/all_gather | solution.py:22
  94.3 70.6 %all-gather.4.cloned.1.call-done = bf16[896,4096]{1,0:T(8,128)(2,1)} async-done(((bf16[896,256]{1,0:T(8,128)(2,1)}), bf16[896,4096]{1,0:T(8,128)(2,1)}) %all-gather.4.cloned.1.call-update) | async-done | bytes 7340048 | tf_op jit(solution)/shard_map/all_gather | solution.py:12
  164.9 6.7 %fusion.9 = (bf16[128,896]{1,0:T(8,128)(2,1)}, bf16[128,896]{1,0:T(8,128)(2,1)}, bf16[128,896]{1,0:T(8,128)(2,1)S(1)}) fusion(bf16[128,896]{1,0:T(8,128)(2,1)} %param.4, bf16[128,896]{1,0:T(8,128)(2,1)} %param.5, bf16[128,4096]{0,1:T(8,128)(2,1)} %all-gather.6.cloned.1.call-done, bf16[896,4096]{1,0:T(8,128)(2,1)} %all-gather.4.cloned.1.call-done), kind=kOutput, calls=%fused_computation.17 | convolution fusion | flops 941588480 | bytes 9535488 | tf_op jit(solution)/shard_map/dot_general | solution.py:23
  171.6 0.0 copy-start
  171.6 0.0 copy-start.1
  171.6 5.9 %convolution_bitcast_fusion = f32[4096,128]{0,1:T(8,128)} fusion(bf16[128,896]{1,0:T(8,128)(2,1)S(1)} %get-tuple-element.6, bf16[896,4096]{1,0:T(8,128)(2,1)} %all-gather.4.cloned.1.call-done), kind=kOutput, calls=%fused_computation | convolution fusion | flops 939524096 | bytes 9666560 | tf_op jit(solution)/shard_map/dot_general | solution.py:14
  177.4 0.0 copy-done
  177.4 0.0 reduce-scatter.2.cloned.1.call-update
  177.5 0.0 all-gather.8.cloned.1.call-start
  177.5 0.5 all-gather.8.cloned.1.call-update
  178.0 0.0 copy-done.1
  178.1 32.2 %all_to_all.19 = bf16[128,16,256]{0,2,1:T(8,128)(2,1)S(1)} all-to-all(bf16[128,16,256]{0,2,1:T(8,128)(2,1)S(1)} %bitcast.14), channel_id=1, replica_groups=mesh['row'=32,'col'=16] {'col'}, dimensions={1} | all-to-all | bytes 2097152 | tf_op jit(solution)/shard_map/all_to_all | solution.py:28
  210.2 0.5 copy.9
  210.8 179.2 %reduce-scatter.2.cloned.1.call-done = f32[128,128]{0,1:T(8,128)} async-done(((f32[4096,128]{0,1:T(8,128)}), f32[128,128]{0,1:T(8,128)}) %reduce-scatter.2.cloned.1.call-update) | async-done | bytes 65552 | tf_op jit(solution)/shard_map/reduce_scatter | solution.py:13
  390.0 1.5 convert_bitcast_fusion
  391.4 50.4 %all-gather.8.cloned.1.call-done = bf16[2048,896]{1,0:T(8,128)(2,1)} async-done(((bf16[128,896]{1,0:T(8,128)(2,1)}), bf16[2048,896]{1,0:T(8,128)(2,1)}) %all-gather.8.cloned.1.call-update) | async-done | bytes 3670032 | tf_op jit(solution)/shard_map/all_gather | solution.py:30
  441.9 4.0 convolution_convert_fusion
Async XLA Ops:
  7.2 87.1 %all-gather.6.cloned.1.call-start = ((), (), s32[]{:S(2)}) async-start(), calls=%async_computation.4 | async-start | bytes 1081344 | tf_op jit(solution)/shard_map/all_gather | solution.py:22
  8.7 156.2 %all-gather.4.cloned.1.call-start = ((), (), s32[]{:S(2)}) async-start(), calls=%async_computation.2 | async-start | bytes 7798784 | tf_op jit(solution)/shard_map/all_gather | solution.py:12
  9.5 380.5 %reduce-scatter.2.cloned.1.call-start = ((), (), s32[]{:S(2)}) async-start(), calls=%async_computation.3 | async-start | bytes 2162688 | tf_op jit(solution)/shard_map/reduce_scatter | solution.py:13
  171.6 5.9 %copy-start = (bf16[128,896]{1,0:T(8,128)(2,1)}, bf16[128,896]{1,0:T(8,128)(2,1)S(1)}, u32[]{:S(2)}) copy-start(bf16[128,896]{1,0:T(8,128)(2,1)S(1)} %get-tuple-element.6) | copy-start | bytes 688132
  171.6 6.5 %copy-start.1 = (bf16[128,4096]{0,1:T(8,128)(2,1)S(1)}, bf16[128,4096]{0,1:T(8,128)(2,1)}, u32[]{:S(2)}) copy-start(bf16[128,4096]{0,1:T(8,128)(2,1)} %all-gather.6.cloned.1.call-done) | copy-start | bytes 3145732
  177.5 264.4 %all-gather.8.cloned.1.call-start = ((), (), s32[]{:S(2)}) async-start(), calls=%async_computation.5 | async-start | bytes 3899392 | tf_op jit(solution)/shard_map/all_gather | solution.py:30
Sparse Core Ops, SparseCore 0:
  11.7 82.4 all-gather.5
  96.3 68.5 all-gather.3
  177.6 212.3 reduce-scatter.1
  392.7 49.0 all-gather.7
where the time goes:
time: 453 us; the launch traced here: 452 us
  waiting for transfers between devices  386 us (85%)
  blocking collectives  32.2 us (7%)
  matrix products  16.5 us (4%)
  between operations  13.8 us (3%)
    reduce_scatter x1, waiting for transfers between devices, body(): lax.psum_scatter(lax.dot_general(weights, hidden, (((0,), (1,)), ((), ())...  179 us
    all_gather x1, waiting for transfers between devices, body(): grad_full = lax.all_gather(out_grad, 'row', axis=1, tiled=True)  84.8 us
    all_gather x1, waiting for transfers between devices, body(): weights = lax.all_gather(down_weight, 'col', axis=1, tiled=True)  70.6 us
    all_gather x1, waiting for transfers between devices, body(): lax.all_gather(hidden, 'col', axis=0, tiled=True)  50.4 us
    all_to_all x1, blocking collectives, body(): lax.all_to_all(grad_full, 'col', split_axis=1, concat_axis=0, tiled=True)  32.2 us
  transfers between devices with their start and end apart: 4, of which 4 were waited for; matrix products, arithmetic and copies ran while one was open for 0% of the time, Pallas kernels for 0%

commit v1 on v0

v1 whole, which is shorter than its diff:
```python
import jax
import jax.numpy as jnp
from jax import lax
from jax.experimental import pallas as pl
from jax.experimental.pallas import tpu as pltpu
from jax.sharding import Mesh, PartitionSpec as P

X, Y, Z, CORES = 4, 8, 8, 2
AXES = ("x", "y", "z", "core")
WHOLE = pl.BlockSpec(memory_space=pltpu.VMEM)
UNREAD = pl.BlockSpec(memory_space=pl.ANY)


def index_of(x, y, z, core):
    return ((x * Y + y) * Z + z) * CORES + core


def to_feature_owner():
    pairs = []
    for x in range(X):
        for y in range(Y):
            for z in range(Z):
                for core in range(CORES):
                    target = index_of((y % 4 + 2 * core) % 4, z, 2 * x + y // 4, core)
                    pairs.append((index_of(x, y, z, core), target))
    return pairs


def kernel_call(kernel, out_shape, in_specs, flops, size):
    return pl.pallas_call(
        kernel,
        out_shape=out_shape,
        in_specs=in_specs,
        out_specs=jax.tree.map(lambda _: WHOLE, out_shape),
        compiler_params=pltpu.CompilerParams(vmem_limit_bytes=40 * 1024 * 1024),
        cost_estimate=pl.CostEstimate(flops=flops, bytes_accessed=size, transcendentals=0),
    )


def hidden_kernel(gate_ref, up_ref, grad_ref, hidden_ref, grad_out_ref):
    gate = gate_ref[...].astype(jnp.float32)
    up = up_ref[...].astype(jnp.float32)
    hidden_ref[...] = (gate * jax.nn.sigmoid(gate) * up).astype(jnp.bfloat16)
    grad_out_ref[...] = grad_ref[...]


def share_kernel(grad_ref, own_ref, other_ref, _, share_ref):
    sub = grad_ref.shape[2]
    total = None
    for q in range(grad_ref.shape[0]):
        weights = (own_ref if q < 2 else other_ref)[:, (q % 2) * sub : (q % 2 + 1) * sub]
        term = lax.dot_general(grad_ref[q], weights, (((1,), (1,)), ((), ())), preferred_element_type=jnp.float32)
        total = term if total is None else total + term
    share_ref[...] = total.astype(jnp.bfloat16)


def output_kernel(hidden_ref, own_ref, other_ref, out_ref):
    sub = out_ref.shape[2]
    for half, weights in enumerate((own_ref, other_ref)):
        product = jnp.dot(hidden_ref[...], weights[...], preferred_element_type=jnp.float32).astype(jnp.bfloat16)
        out_ref[2 * half] = product[:, :sub]
        out_ref[2 * half + 1] = product[:, sub:]


def weight_grad_kernel(hidden_ref, grad_ref, _, own_ref, other_ref):
    sub = grad_ref.shape[2]
    for q in range(grad_ref.shape[0]):
        target = own_ref if q < 2 else other_ref
        target[:, (q % 2) * sub : (q % 2 + 1) * sub] = lax.dot_general(
            hidden_ref[...], grad_ref[q], (((0,), (0,)), ((), ())), preferred_element_type=jnp.float32
        )


def sum_kernel(parts_ref, sum_ref):
    total = parts_ref[0].astype(jnp.float32)
    for i in range(1, parts_ref.shape[0]):
        total = total + parts_ref[i].astype(jnp.float32)
    sum_ref[...] = total.astype(jnp.bfloat16)


def add_kernel(a_ref, b_ref, sum_ref):
    sum_ref[...] = (a_ref[...] + b_ref[...]).astype(jnp.bfloat16)


def gradient_kernel(hidden_grad_ref, gate_ref, up_ref, gate_grad_ref, up_grad_ref):
    hidden_grad = hidden_grad_ref[...].astype(jnp.float32)
    gate = gate_ref[...].astype(jnp.float32)
    up = up_ref[...].astype(jnp.float32)
    sigmoid = jax.nn.sigmoid(gate)
    gate_grad_ref[...] = (hidden_grad * up * sigmoid * (1.0 + gate * (1.0 - sigmoid))).astype(jnp.bfloat16)
    up_grad_ref[...] = (hidden_grad * gate * sigmoid).astype(jnp.bfloat16)


def body(gate_pre, up_pre, down_weight, out_grad):
    bf16, f32, shape = jnp.bfloat16, jnp.float32, jax.ShapeDtypeStruct
    there = to_feature_owner()
    back = [(b, a) for a, b in there]
    tokens, units = gate_pre.shape
    sub, features = out_grad.shape[1], down_weight.shape[1]
    rows = Z * tokens
    flops = 2 * rows * units * CORES * features
    swap = [(0, 1), (1, 0)]

    hidden, grad = kernel_call(
        hidden_kernel, (shape((tokens, units), bf16), shape(out_grad.shape, bf16)), [WHOLE] * 3, 0, 6 * tokens * units
    )(gate_pre, up_pre, out_grad)
    hidden_all = lax.all_gather(hidden, "z", axis=0, tiled=True)
    other_weight = lax.ppermute(down_weight, "core", swap)

    grad = lax.ppermute(grad, AXES, there)
    grad = lax.all_to_all(jnp.broadcast_to(grad, (Y, tokens, sub)), "y", split_axis=0, concat_axis=0, tiled=True)
    grad = jnp.broadcast_to(grad.reshape(rows, sub), (X, rows, sub))
    grad = lax.all_to_all(grad, "x", split_axis=0, concat_axis=0, tiled=True)

    share = kernel_call(
        share_kernel, shape((rows, units), bf16), [WHOLE, WHOLE, WHOLE, UNREAD], flops, 4 * rows * units
    )(grad, down_weight, other_weight, hidden_all)
    hidden_grad = lax.psum_scatter(share, "z", scatter_dimension=0, tiled=True)
    gate_grad, up_grad = kernel_call(
        gradient_kernel, (shape((tokens, units), bf16),) * 2, [WHOLE] * 3, 0, 10 * tokens * units
    )(hidden_grad, gate_pre, up_pre)

    output = kernel_call(output_kernel, shape((X, rows, sub), bf16), [WHOLE] * 3, flops, 4 * rows * units)(
        hidden_all, down_weight, other_weight
    )
    output = lax.all_to_all(output, "x", split_axis=0, concat_axis=0, tiled=True)
    output = kernel_call(sum_kernel, shape((rows, sub), bf16), [WHOLE], 0, 10 * rows * sub)(output)
    output = lax.all_to_all(output.reshape(Y, tokens, sub), "y", split_axis=0, concat_axis=0, tiled=True)
    output_sum = kernel_call(sum_kernel, shape((tokens, sub), bf16), [WHOLE], 0, 18 * tokens * sub)(output)
    output = lax.ppermute(output_sum, AXES, back)

    own, other = kernel_call(
        weight_grad_kernel, (shape((units, features), f32),) * 2, [WHOLE, WHOLE, UNREAD], flops, 4 * rows * units
    )(hidden_all, grad, output_sum)
    weight_grad = kernel_call(add_kernel, shape((units, features), bf16), [WHOLE] * 2, 0, 10 * units * features)(
        own, lax.ppermute(other, "core", swap)
    )
    return output, gate_grad, up_grad, weight_grad


def solution(mesh):
    chips = Mesh(mesh.devices.reshape(X, Y, Z, CORES), AXES)
    by_token = P(("z", "core"), ("x", "y"))
    by_unit = P(("x", "y"), ("z", "core"))
    return jax.shard_map(
        body,
        mesh=chips,
        in_specs=(by_token, by_token, by_unit, by_token),
        out_specs=(by_token, by_token, by_token, by_unit),
        check_vma=False,
    )
```

time: 453 us -> 131 us (0.29)
  the two profiles are of different devices: /device:TPU:1 before, /device:TPU:46 now
where the time goes in v1:
time: 131 us
  blocking collectives  43.6 us (33%)
  starting transfers between devices  30.8 us (24%)
  waiting for transfers between devices  22.6 us (17%)
  between operations  14.1 us (11%)
  local copies, waits for them, and re-layouts  10.1 us (8%)
  Pallas kernels  9.4 us (7%)
    all_to_all x1, blocking collectives, body(): lax.all_to_all(output, 'x', split_axis=0, concat_axis=0, tiled=True)  15.6 us
    all_to_all x1, blocking collectives, body(): lax.all_to_all(jnp.broadcast_to(grad, (Y, tokens, sub)), 'y', split_axis=...  15.3 us
    all_to_all x1, blocking collectives, body(): lax.all_to_all(output.reshape(Y, tokens, sub), 'y', split_axis=0, concat_...  12.7 us
    ppermute x1, starting transfers between devices, body(): grad = lax.ppermute(grad, AXES, there)  11.2 us
    ppermute x1, starting transfers between devices, body(): output = lax.ppermute(output_sum, AXES, back)  10.2 us
    ppermute x1, waiting for transfers between devices, body(): output = lax.ppermute(output_sum, AXES, back)  9.28 us
    unnamed x23, local copies, waits for them, and re-layouts  8.95 us
    all_to_all x1, waiting for transfers between devices, body(): grad = lax.all_to_all(grad, 'x', split_axis=0, concat_axis=0, tiled=True)  8.42 us
  transfers between devices with their start and end apart: 7, of which 5 were waited for; matrix products, arithmetic and copies ran while one was open for 1% of the time, Pallas kernels for 3%

profile of v1, /device:TPU:46, one launch (start us, length us, event | category | flops | bytes accessed | tf_op | source)
XLA Modules:
  0.0 130.6 jit_solution(18223638411206073120)
XLA Ops:
  7.2 0.0 all-gather.2.cloned.1.call-start
  7.2 0.0 copy-start.5
  7.2 0.9 copy-done.5
  8.2 0.0 copy-start.7
  8.2 0.9 copy-done.7
  9.1 0.0 copy-start.10
  9.1 0.8 copy-done.10
  9.8 0.8 shard_map.75
  10.6 0.0 all-gather.2.cloned.1.call-update
  10.7 11.2 %collective-permute-start.2 = (bf16[128,128]{1,0:T(8,128)(2,1)S(1)}, bf16[128,128]{1,0:T(8,128)(2,1)S(1)}, u32[]{:S(2)}, u32[]{:S(2)}) collective-permute-start(bf16[128,128]{1,0:T(8,128)(2,1)S(1)} %get-tuple-element.11), channel_id=1, source_target_pairs={{0,0},{1,257},{2,16},{3,273},{4,32},{5,289},{6,48},{7,305},{8,64},... | collective-permute-start | bytes 98312 | tf_op jit(solution)/shard_map/ppermute | solution.py:110
  21.9 3.0 %collective-permute-done.2 = bf16[128,128]{1,0:T(8,128)(2,1)S(1)} collective-permute-done((bf16[128,128]{1,0:T(8,128)(2,1)S(1)}, bf16[128,128]{1,0:T(8,128)(2,1)S(1)}, u32[]{:S(2)}, u32[]{:S(2)}) %collective-permute-start.2) | collective-permute-done | bytes 32800 | tf_op jit(solution)/shard_map/ppermute | solution.py:110
  24.9 15.3 %all_to_all.20 = bf16[8,128,128]{2,1,0:T(8,128)(2,1)S(1)} all-to-all(bf16[8,128,128]{2,1,0:T(8,128)(2,1)S(1)} %broadcast_in_dim.6), channel_id=1, replica_groups=mesh['x'=4,'y'=8,'z'=8,'core'=2] {'y'}, dimensions={0} | all-to-all | bytes 524288 | tf_op jit(solution)/shard_map/all_to_all | solution.py:111
  40.2 0.0 copy-start.2
  40.2 1.1 broadcast_in_dim.7
  41.3 5.4 %all-to-all-start.3 = ((bf16[4,1024,128]{2,1,0:T(8,128)(2,1)}), bf16[4,1024,128]{2,1,0:T(8,128)(2,1)S(1)}, u32[]{:S(2)}, u32[]{:S(2)}) async-start(bf16[4,1024,128]{2,1,0:T(8,128)(2,1)} %broadcast_in_dim.7), calls=%async_computation.3 | async-start | bytes 2097152 | tf_op jit(solution)/shard_map/all_to_all | solution.py:113
  46.7 0.0 reduce-scatter.2.cloned.1.call-start
  46.7 0.0 copy-done.2
  46.7 1.9 %collective-permute-start = (bf16[896,256]{1,0:T(8,128)(2,1)S(1)}, bf16[896,256]{1,0:T(8,128)(2,1)S(1)}, u32[]{:S(2)}, u32[]{:S(2)}) collective-permute-start(bf16[896,256]{1,0:T(8,128)(2,1)S(1)} %copy-done.2), channel_id=1, source_target_pairs={{0,1},{1,0},{2,3},{3,2},{4,5},{5,4},{6,7},{7,6},{8,9},{9,8},{10,11... | collective-permute-start | bytes 1376264 | tf_op jit(solution)/shard_map/ppermute | solution.py:108
  48.6 1.8 %collective-permute-done.other_ref = bf16[896,256]{1,0:T(8,128)(2,1)S(1)} collective-permute-done((bf16[896,256]{1,0:T(8,128)(2,1)S(1)}, bf16[896,256]{1,0:T(8,128)(2,1)S(1)}, u32[]{:S(2)}, u32[]{:S(2)}) %collective-permute-start) | collective-permute-done | bytes 458784 | tf_op jit(solution)/shard_map/ppermute | solution.py:108
  50.4 8.4 %all-to-all-done.3.grad_ref = bf16[4,1024,128]{2,1,0:T(8,128)(2,1)S(1)} async-done(((bf16[4,1024,128]{2,1,0:T(8,128)(2,1)}), bf16[4,1024,128]{2,1,0:T(8,128)(2,1)S(1)}, u32[]{:S(2)}, u32[]{:S(2)}) %all-to-all-start.3) | async-done | bytes 1048608 | tf_op jit(solution)/shard_map/all_to_all | solution.py:113
  58.8 0.1 all-gather.2.cloned.1.call-done.hidden_ref._
  58.9 0.0 copy-start
  58.9 1.5 %copy-done = bf16[1024,896]{1,0:T(8,128)(2,1)S(1)} copy-done((bf16[1024,896]{1,0:T(8,128)(2,1)S(1)}, bf16[1024,896]{1,0:T(8,128)(2,1)}, u32[]{:S(2)}) %copy-start) | copy-done | bytes 1835032
  60.4 3.3 %shard_map.79 = bf16[1024,896]{1,0:T(8,128)(2,1)} custom-call(bf16[4,1024,128]{2,1,0:T(8,128)(2,1)S(1)} %all-to-all-done.3.grad_ref, bf16[896,256]{1,0:T(8,128)(2,1)S(1)} %copy-done.2, bf16[896,256]{1,0:T(8,128)(2,1)S(1)} %collective-permute-done.other_ref, bf16[1024,896]{1,0:T(8,128)(2,1)S(1)} %copy-done), custom_call_target="tpu_custom_call" | custom-call | flops 939524096 | bytes 3670016 | tf_op jit(solution)/shard_map/pallas_call | solution.py:115
  63.7 0.0 copy-start.3
  63.7 0.8 copy-done.3
  64.4 0.0 copy-start.1
  64.4 0.0 reduce-scatter.2.cloned.1.call-update
  64.5 1.5 %copy-done.1 = bf16[1024,896]{1,0:T(8,128)(2,1)S(1)} copy-done((bf16[1024,896]{1,0:T(8,128)(2,1)S(1)}, bf16[1024,896]{1,0:T(8,128)(2,1)}, u32[]{:S(2)}) %copy-start.1) | copy-done | bytes 1835032
  65.9 0.0 copy-start.4
  65.9 1.0 copy-done.4
  67.0 1.2 shard_map.76
  68.2 15.6 %all_to_all.21.parts_ref = bf16[4,1024,128]{2,1,0:T(8,128)(2,1)S(1)} all-to-all(bf16[4,1024,128]{2,1,0:T(8,128)(2,1)S(1)} %shard_map.76), channel_id=1, replica_groups=mesh['x'=4,'y'=8,'z'=8,'core'=2] {'x'}, dimensions={0} | all-to-all | bytes 2097152 | tf_op jit(solution)/shard_map/all_to_all | solution.py:126
  83.8 0.1 shard_map.77
  83.9 12.7 %all_to_all.22.parts_ref = bf16[8,128,128]{2,1,0:T(8,128)(2,1)S(1)} all-to-all(bf16[8,128,128]{2,1,0:T(8,128)(2,1)S(1)} %bitcast.2), channel_id=1, replica_groups=mesh['x'=4,'y'=8,'z'=8,'core'=2] {'y'}, dimensions={0} | all-to-all | bytes 524288 | tf_op jit(solution)/shard_map/all_to_all | solution.py:128
  96.7 2.1 %shard_map.81 = (f32[896,256]{1,0:T(8,128)S(1)}, f32[896,256]{1,0:T(8,128)S(1)}) custom-call(bf16[1024,896]{1,0:T(8,128)(2,1)S(1)} %copy-done.1, bf16[4,1024,128]{2,1,0:T(8,128)(2,1)S(1)} %all-to-all-done.3.grad_ref, bf16[128,128]{1,0:T(8,128)(2,1)S(1)} %shard_map.78._), custom_call_target="tpu_custom_call" | custom-call | flops 939524096 | bytes 3670016 | tf_op jit(solution)/shard_map/pallas_call | solution.py:132
  98.8 0.0 copy-start.6
  98.8 0.0 copy-start.8
  98.8 2.1 %collective-permute-start.3 = (f32[896,256]{1,0:T(8,128)S(1)}, f32[896,256]{1,0:T(8,128)S(1)}, u32[]{:S(2)}, u32[]{:S(2)}) collective-permute-start(f32[896,256]{1,0:T(8,128)S(1)} %get-tuple-element.15), channel_id=1, source_target_pairs={{0,1},{1,0},{2,3},{3,2},{4,5},{5,4},{6,7},{7,6},{8,9},{9,8},{10,11... | collective-permute-start | bytes 2752520 | tf_op jit(solution)/shard_map/ppermute | solution.py:136
  100.9 10.2 %collective-permute-start.1 = (bf16[128,128]{1,0:T(8,128)(2,1)S(1)}, bf16[128,128]{1,0:T(8,128)(2,1)S(1)}, u32[]{:S(2)}, u32[]{:S(2)}) collective-permute-start(bf16[128,128]{1,0:T(8,128)(2,1)S(1)} %shard_map.78._), channel_id=1, source_target_pairs={{0,0},{257,1},{16,2},{273,3},{32,4},{289,5},{48,6},{305,7},{64,8},... | collective-permute-start | bytes 98312 | tf_op jit(solution)/shard_map/ppermute | solution.py:130
  111.1 9.3 %collective-permute-done.1 = bf16[128,128]{1,0:T(8,128)(2,1)S(1)} collective-permute-done((bf16[128,128]{1,0:T(8,128)(2,1)S(1)}, bf16[128,128]{1,0:T(8,128)(2,1)S(1)}, u32[]{:S(2)}, u32[]{:S(2)}) %collective-permute-start.1) | collective-permute-done | bytes 32800 | tf_op jit(solution)/shard_map/ppermute | solution.py:130
  120.4 0.0 collective-permute-done.3.b_ref
  120.4 0.8 shard_map.82
  121.2 0.0 reduce-scatter.2.cloned.1.call-done.hidden_grad_ref
  121.2 0.0 copy-done.6
  121.2 0.0 copy-done.8
  121.2 0.0 copy-start.9
  121.3 0.9 copy-done.9
  122.2 0.9 shard_map.80
  123.1 0.6 copy.9
  (2 shorter events, 0.1 us)
Async XLA Ops:
  7.2 51.7 %all-gather.2.cloned.1.call-start = ((), (), s32[]{:S(2)}) async-start(), calls=%async_computation.5 | async-start | bytes 2064384 | tf_op jit(solution)/shard_map/all_gather | solution.py:107
  7.2 0.9 copy-start.5
  8.2 0.9 copy-start.7
  9.1 0.8 copy-start.10
  10.7 14.2 %collective-permute-start.2 = (bf16[128,128]{1,0:T(8,128)(2,1)S(1)}, bf16[128,128]{1,0:T(8,128)(2,1)S(1)}, u32[]{:S(2)}, u32[]{:S(2)}) collective-permute-start(bf16[128,128]{1,0:T(8,128)(2,1)S(1)} %get-tuple-element.11), channel_id=1, source_target_pairs={{0,0},{1,257},{2,16},{3,273},{4,32},{5,289},{6,48},{7,305},{8,64},... | collective-permute-start | bytes 98312 | tf_op jit(solution)/shard_map/ppermute | solution.py:110
  40.2 6.5 %copy-start.2 = (bf16[896,256]{1,0:T(8,128)(2,1)S(1)}, bf16[896,256]{1,0:T(8,128)(2,1)}, u32[]{:S(2)}) copy-start(bf16[896,256]{1,0:T(8,128)(2,1)} %own_ref.3) | copy-start | bytes 1376260
  41.3 17.5 %all-to-all-start.3 = ((bf16[4,1024,128]{2,1,0:T(8,128)(2,1)}), bf16[4,1024,128]{2,1,0:T(8,128)(2,1)S(1)}, u32[]{:S(2)}, u32[]{:S(2)}) async-start(bf16[4,1024,128]{2,1,0:T(8,128)(2,1)} %broadcast_in_dim.7), calls=%async_computation.3 | async-start | bytes 2097152 | tf_op jit(solution)/shard_map/all_to_all | solution.py:113
  46.7 74.6 %reduce-scatter.2.cloned.1.call-start = ((), (), s32[]{:S(2)}) async-start(), calls=%async_computation.6 | async-start | bytes 2064384 | tf_op jit(solution)/shard_map/reduce_scatter | solution.py:118
  46.7 3.7 %collective-permute-start = (bf16[896,256]{1,0:T(8,128)(2,1)S(1)}, bf16[896,256]{1,0:T(8,128)(2,1)S(1)}, u32[]{:S(2)}, u32[]{:S(2)}) collective-permute-start(bf16[896,256]{1,0:T(8,128)(2,1)S(1)} %copy-done.2), channel_id=1, source_target_pairs={{0,1},{1,0},{2,3},{3,2},{4,5},{5,4},{6,7},{7,6},{8,9},{9,8},{10,11... | collective-permute-start | bytes 1376264 | tf_op jit(solution)/shard_map/ppermute | solution.py:108
  58.9 1.5 %copy-start = (bf16[1024,896]{1,0:T(8,128)(2,1)S(1)}, bf16[1024,896]{1,0:T(8,128)(2,1)}, u32[]{:S(2)}) copy-start(bf16[1024,896]{1,0:T(8,128)(2,1)} %all-gather.2.cloned.1.call-done.hidden_ref._) | copy-start | bytes 5505028
  63.7 0.8 copy-start.3
  64.4 1.5 %copy-start.1 = (bf16[1024,896]{1,0:T(8,128)(2,1)S(1)}, bf16[1024,896]{1,0:T(8,128)(2,1)}, u32[]{:S(2)}) copy-start(bf16[1024,896]{1,0:T(8,128)(2,1)} %all-gather.2.cloned.1.call-done.hidden_ref._) | copy-start | bytes 5505028
  65.9 1.0 copy-start.4
  98.8 22.4 %copy-start.6 = (bf16[128,896]{1,0:T(8,128)(2,1)S(1)}, bf16[128,896]{1,0:T(8,128)(2,1)}, u32[]{:S(2)}) copy-start(bf16[128,896]{1,0:T(8,128)(2,1)} %gate_ref.3) | copy-start | bytes 688132
  98.8 22.4 %copy-start.8 = (bf16[128,896]{1,0:T(8,128)(2,1)S(1)}, bf16[128,896]{1,0:T(8,128)(2,1)}, u32[]{:S(2)}) copy-start(bf16[128,896]{1,0:T(8,128)(2,1)} %up_ref.3) | copy-start | bytes 688132
  98.8 21.5 %collective-permute-start.3 = (f32[896,256]{1,0:T(8,128)S(1)}, f32[896,256]{1,0:T(8,128)S(1)}, u32[]{:S(2)}, u32[]{:S(2)}) collective-permute-start(f32[896,256]{1,0:T(8,128)S(1)} %get-tuple-element.15), channel_id=1, source_target_pairs={{0,1},{1,0},{2,3},{3,2},{4,5},{5,4},{6,7},{7,6},{8,9},{9,8},{10,11... | collective-permute-start | bytes 2752520 | tf_op jit(solution)/shard_map/ppermute | solution.py:136
  100.9 19.5 %collective-permute-start.1 = (bf16[128,128]{1,0:T(8,128)(2,1)S(1)}, bf16[128,128]{1,0:T(8,128)(2,1)S(1)}, u32[]{:S(2)}, u32[]{:S(2)}) collective-permute-start(bf16[128,128]{1,0:T(8,128)(2,1)S(1)} %shard_map.78._), channel_id=1, source_target_pairs={{0,0},{257,1},{16,2},{273,3},{32,4},{289,5},{48,6},{305,7},{64,8},... | collective-permute-start | bytes 98312 | tf_op jit(solution)/shard_map/ppermute | solution.py:130
  121.2 0.9 copy-start.9
Sparse Core Ops, SparseCore 0:
  10.8 48.0 all-gather.1
  64.6 46.0 reduce-scatter.1

commit v2 on v1

v2 whole, which is shorter than its diff:
```python
import jax
import jax.numpy as jnp
from jax import lax
from jax.experimental import pallas as pl
from jax.experimental.pallas import tpu as pltpu
from jax.sharding import Mesh, PartitionSpec as P

X, Y, Z, CORES = 4, 8, 8, 2
AXES = ("x", "y", "z", "core")
def index_of(x, y, z, core):
    return ((x * Y + y) * Z + z) * CORES + core


def to_feature_owner():
    pairs = []
    for x in range(X):
        for y in range(Y):
            for z in range(Z):
                for core in range(CORES):
                    target = index_of((y % 4 + 2 * core) % 4, z, 2 * x + y // 4, core)
                    pairs.append((index_of(x, y, z, core), target))
    return pairs


def kernel_call(kernel, out_shape, flops, size, vmem=24, **more):
    return pl.pallas_call(
        kernel,
        out_shape=out_shape,
        compiler_params=pltpu.CompilerParams(vmem_limit_bytes=vmem * 1024 * 1024),
        cost_estimate=pl.CostEstimate(flops=flops, bytes_accessed=size, transcendentals=0),
        **more,
    )


def streamed_call(kernel, out_shape, flops, size, scratch_shapes):
    in_hbm = pl.BlockSpec(memory_space=pl.ANY)

    def call(*arrays):
        return kernel_call(
            kernel,
            out_shape,
            flops,
            size,
            vmem=60,
            in_specs=[in_hbm] * len(arrays),
            out_specs=jax.tree.map(lambda _: in_hbm, out_shape),
            scratch_shapes=scratch_shapes,
        )(*arrays)

    return call


def started(source, target, sem):
    copy = pltpu.make_async_copy(source, target, sem)
    copy.start()
    return copy


def hidden_kernel(gate_ref, up_ref, hidden_ref, gate_in, up_in, hidden_out, sems):
    copies = [started(gate_ref, gate_in, sems.at[0]), started(up_ref, up_in, sems.at[1])]
    for copy in copies:
        copy.wait()
    gate = gate_in[...].astype(jnp.float32)
    up = up_in[...].astype(jnp.float32)
    hidden_out[...] = (gate * jax.nn.sigmoid(gate) * up).astype(jnp.bfloat16)
    started(hidden_out, hidden_ref, sems.at[2]).wait()


def share_kernel(grad_ref, own_ref, other_ref, share_ref, mine_ref):
    z_blocks, tokens, _ = share_ref.shape
    weights = jnp.concatenate([own_ref[...], other_ref[...]], axis=1)

    def product(grad):
        return lax.dot_general(grad, weights, (((1,), (1,)), ((), ())), preferred_element_type=jnp.float32)

    grad = jnp.concatenate([grad_ref[q].reshape(z_blocks * tokens, -1) for q in range(X)], axis=1)
    share_ref[...] = product(grad).astype(jnp.bfloat16).reshape(share_ref.shape)
    here = lax.axis_index("z")
    share_ref[here] = jnp.zeros(mine_ref.shape, jnp.bfloat16)
    mine_ref[...] = product(jnp.concatenate([grad_ref[q, here] for q in range(X)], axis=1))


def output_kernel(hidden_ref, own_ref, other_ref, out_ref):
    _, z_blocks, tokens, sub = out_ref.shape
    for half, weights in enumerate((own_ref, other_ref)):
        product = jnp.dot(hidden_ref[...], weights[...], preferred_element_type=jnp.float32).astype(jnp.bfloat16)
        for h in range(2):
            out_ref[2 * half + h] = product[:, h * sub : (h + 1) * sub].reshape(z_blocks, tokens, sub)


def weight_grad_kernel(hidden_ref, grad_ref, own_ref, other_ref):
    rows = hidden_ref.shape[0]
    for half, out_ref in enumerate((own_ref, other_ref)):
        grad = jnp.concatenate([grad_ref[2 * half + h].reshape(rows, -1) for h in range(2)], axis=1)
        out_ref[...] = lax.dot_general(
            hidden_ref[...], grad, (((0,), (0,)), ((), ())), preferred_element_type=jnp.float32
        ).astype(out_ref.dtype)


def sum_kernel(parts_ref, sum_ref):
    total = parts_ref[0].astype(jnp.float32)
    for i in range(1, parts_ref.shape[0]):
        total = total + parts_ref[i].astype(jnp.float32)
    sum_ref[...] = total.astype(jnp.bfloat16)


def add_kernel(a_ref, b_ref, sum_ref):
    sum_ref[...] = (a_ref[...] + b_ref[...]).astype(jnp.bfloat16)


def gradient_kernel(mine_ref, others_ref, gate_ref, up_ref, gate_grad_ref, up_grad_ref):
    hidden_grad = mine_ref[...] + others_ref[...].astype(jnp.float32)
    gate = gate_ref[...].astype(jnp.float32)
    up = up_ref[...].astype(jnp.float32)
    sigmoid = jax.nn.sigmoid(gate)
    gate_grad_ref[...] = (hidden_grad * up * sigmoid * (1.0 + gate * (1.0 - sigmoid))).astype(jnp.bfloat16)
    up_grad_ref[...] = (hidden_grad * gate * sigmoid).astype(jnp.bfloat16)


def body(gate_pre, up_pre, down_weight, out_grad):
    bf16, f32, shape = jnp.bfloat16, jnp.float32, jax.ShapeDtypeStruct
    there = to_feature_owner()
    back = [(b, a) for a, b in there]
    tokens, units = gate_pre.shape
    sub, features = out_grad.shape[1], down_weight.shape[1]
    rows = Z * tokens
    flops = 2 * rows * units * CORES * features
    swap = [(0, 1), (1, 0)]
    together = lax.optimization_barrier

    def exchanged(array, axis):
        return lax.all_to_all(array, axis, split_axis=0, concat_axis=0, tiled=True)

    block = (tokens, units)
    vmem, dma = pltpu.VMEM, pltpu.SemaphoreType.DMA
    hidden = streamed_call(
        hidden_kernel, shape(block, bf16), 0, 6 * tokens * units, [vmem(block, bf16)] * 3 + [dma((3,))]
    )(gate_pre, up_pre)
    hidden, out_grad = together((hidden, out_grad))
    hidden_all = lax.all_gather(hidden, "z", axis=0, tiled=True)

    grad = lax.ppermute(out_grad, AXES, there)
    other_weight = lax.ppermute(down_weight, "core", swap)
    grad = exchanged(jnp.broadcast_to(grad, (Y, tokens, sub)), "y")
    grad = exchanged(jnp.broadcast_to(grad, (X, Y, tokens, sub)), "x")

    output = kernel_call(output_kernel, shape((X, Y, tokens, sub), bf16), flops, 4 * rows * units)(
        hidden_all, down_weight, other_weight
    )
    output, grad = together((output, grad))

    share, mine = kernel_call(
        share_kernel, (shape((Z, tokens, units), bf16), shape(block, f32)), flops, 4 * rows * units
    )(grad, down_weight, other_weight)
    others = lax.psum_scatter(share.reshape(rows, units), "z", scatter_dimension=0, tiled=True)
    gate_grad, up_grad = kernel_call(gradient_kernel, (shape(block, bf16),) * 2, 0, 14 * tokens * units)(
        mine, others, gate_pre, up_pre
    )

    output = exchanged(output, "x")
    output = kernel_call(sum_kernel, shape((Y, tokens, sub), bf16), 0, 10 * rows * sub)(output)
    output = exchanged(output, "y")
    output = kernel_call(sum_kernel, shape((tokens, sub), bf16), 0, 18 * tokens * sub)(output)
    output = lax.ppermute(output, AXES, back)
    output, gate_grad, up_grad = together((output, gate_grad, up_grad))

    own, other = kernel_call(
        weight_grad_kernel, (shape((units, features), f32),) * 2, flops, 4 * rows * units
    )(hidden_all, grad)
    weight_grad = kernel_call(add_kernel, shape((units, features), bf16), 0, 10 * units * features)(
        own, lax.ppermute(other, "core", swap)
    )
    return output, gate_grad, up_grad, weight_grad


def solution(mesh):
    chips = Mesh(mesh.devices.reshape(X, Y, Z, CORES), AXES)
    by_token = P(("z", "core"), ("x", "y"))
    by_unit = P(("x", "y"), ("z", "core"))
    return jax.shard_map(
        body,
        mesh=chips,
        in_specs=(by_token, by_token, by_unit, by_token),
        out_specs=(by_token, by_token, by_token, by_unit),
        check_vma=False,
    )
```

time: 131 us -> 120 us (0.916)
  the two profiles are of different devices: /device:TPU:46 before, /device:TPU:36 now
where the time goes in v2:
time: 120 us
  starting transfers between devices  33.3 us (28%)
  waiting for transfers between devices  28.6 us (24%)
  blocking collectives  26.3 us (22%)
  between operations  14.1 us (12%)
  Pallas kernels  10.8 us (9%)
  local copies, waits for them, and re-layouts  6.51 us (5%)
    all_to_all x2, blocking collectives, exchanged(): return lax.all_to_all(array, axis, split_axis=0, concat_axis=0, tiled=True)  26.3 us
    ppermute x1, starting transfers between devices, body(): grad = lax.ppermute(out_grad, AXES, there)  10.4 us
    all_gather x1, waiting for transfers between devices, body(): hidden_all = lax.all_gather(hidden, 'z', axis=0, tiled=True)  10.3 us
    all_to_all x2, starting transfers between devices, exchanged(): return lax.all_to_all(array, axis, split_axis=0, concat_axis=0, tiled=True)  9.74 us
    reduce_scatter x1, waiting for transfers between devices, body(): lax.psum_scatter(share.reshape(rows, units), 'z', scatter_dimension=0, ti...  9.22 us
    ppermute x1, starting transfers between devices, body(): output = lax.ppermute(output, AXES, back)  9.13 us
    ppermute x1, waiting for transfers between devices, body(): grad = lax.ppermute(out_grad, AXES, there)  5.66 us
    unnamed x21, local copies, waits for them, and re-layouts  5.24 us
  transfers between devices with their start and end apart: 8, of which 5 were waited for; matrix products, arithmetic and copies ran while one was open for 1% of the time, Pallas kernels for 5%

profile of v2, /device:TPU:36, one launch (start us, length us, event | category | flops | bytes accessed | tf_op | source)
XLA Modules:
  0.0 119.7 jit_solution(6763895233763221103)
XLA Ops:
  7.2 0.0 all-gather.2.cloned.1.call-start
  7.2 1.9 %shard_map.75 = bf16[128,896]{1,0:T(8,128)(2,1)} custom-call(bf16[128,896]{1,0:T(8,128)(2,1)} %gate_ref.3, bf16[128,896]{1,0:T(8,128)(2,1)} %up_ref.3), custom_call_target="tpu_custom_call" | custom-call | bytes 688128 | tf_op jit(solution)/shard_map/pallas_call | solution.py:39
  9.1 0.0 all-gather.2.cloned.1.call-update
  9.1 10.4 %collective-permute-start.1 = (bf16[128,128]{1,0:T(8,128)(2,1)}, bf16[128,128]{1,0:T(8,128)(2,1)S(1)}, u32[]{:S(2)}, u32[]{:S(2)}) collective-permute-start(bf16[128,128]{1,0:T(8,128)(2,1)} %param.7), channel_id=1, source_target_pairs={{0,0},{1,257},{2,16},{3,273},{4,32},{5,289},{6,48},{7,305},{8,64},... | collective-permute-start | bytes 98312 | tf_op jit(solution)/shard_map/ppermute | solution.py:142
  19.5 5.7 %collective-permute-done.1 = bf16[128,128]{1,0:T(8,128)(2,1)S(1)} collective-permute-done((bf16[128,128]{1,0:T(8,128)(2,1)}, bf16[128,128]{1,0:T(8,128)(2,1)S(1)}, u32[]{:S(2)}, u32[]{:S(2)}) %collective-permute-start.1) | collective-permute-done | bytes 32800 | tf_op jit(solution)/shard_map/ppermute | solution.py:142
  25.2 0.0 copy-start.8
  25.2 13.6 %all_to_all.20 = bf16[8,128,128]{2,1,0:T(8,128)(2,1)S(1)} all-to-all(bf16[8,128,128]{2,1,0:T(8,128)(2,1)S(1)} %broadcast_in_dim.6), channel_id=1, replica_groups=mesh['x'=4,'y'=8,'z'=8,'core'=2] {'y'}, dimensions={0} | all-to-all | bytes 524288 | tf_op jit(solution)/shard_map/all_to_all | solution.py:132
  38.8 1.2 %broadcast_in_dim.7 = bf16[4,8,128,128]{3,2,1,0:T(8,128)(2,1)} broadcast(bf16[8,128,128]{2,1,0:T(8,128)(2,1)S(1)} %all_to_all.20), dimensions={1,2,3} | broadcast | bytes 1310720 | tf_op jit(solution)/shard_map/broadcast_in_dim | solution.py:145
  40.0 4.8 %all-to-all-start.1 = ((bf16[4,8,128,128]{3,2,1,0:T(8,128)(2,1)}), bf16[4,8,128,128]{3,2,1,0:T(8,128)(2,1)S(1)}, u32[]{:S(2)}, u32[]{:S(2)}) async-start(bf16[4,8,128,128]{3,2,1,0:T(8,128)(2,1)} %broadcast_in_dim.7), calls=%async_computation.1 | async-start | bytes 2097152 | tf_op jit(solution)/shard_map/all_to_all | solution.py:132
  44.8 0.0 reduce-scatter.2.cloned.1.call-start
  44.8 0.0 copy-done.8
  44.8 1.9 %collective-permute-start = (bf16[896,256]{1,0:T(8,128)(2,1)S(1)}, bf16[896,256]{1,0:T(8,128)(2,1)S(1)}, u32[]{:S(2)}, u32[]{:S(2)}) collective-permute-start(bf16[896,256]{1,0:T(8,128)(2,1)S(1)} %copy-done.8), channel_id=1, source_target_pairs={{0,1},{1,0},{2,3},{3,2},{4,5},{5,4},{6,7},{7,6},{8,9},{9,8},{10,11... | collective-permute-start | bytes 1376264 | tf_op jit(solution)/shard_map/ppermute | solution.py:143
  46.8 1.8 %collective-permute-done.other_ref = bf16[896,256]{1,0:T(8,128)(2,1)S(1)} collective-permute-done((bf16[896,256]{1,0:T(8,128)(2,1)S(1)}, bf16[896,256]{1,0:T(8,128)(2,1)S(1)}, u32[]{:S(2)}, u32[]{:S(2)}) %collective-permute-start) | collective-permute-done | bytes 458784 | tf_op jit(solution)/shard_map/ppermute | solution.py:143
  48.5 10.3 %all-gather.2.cloned.1.call-done.hidden_ref = bf16[1024,896]{1,0:T(8,128)(2,1)} async-done(((bf16[128,896]{1,0:T(8,128)(2,1)}), bf16[1024,896]{1,0:T(8,128)(2,1)}) %all-gather.2.cloned.1.call-update) | async-done | bytes 1835024 | tf_op jit(solution)/shard_map/all_gather | solution.py:140
  58.9 0.0 copy-start
  58.9 1.5 %copy-done = bf16[1024,896]{1,0:T(8,128)(2,1)S(1)} copy-done((bf16[1024,896]{1,0:T(8,128)(2,1)S(1)}, bf16[1024,896]{1,0:T(8,128)(2,1)}, u32[]{:S(2)}) %copy-start) | copy-done | bytes 1835032
  60.4 2.2 %shard_map.76 = bf16[4,8,128,128]{3,2,1,0:T(8,128)(2,1)} custom-call(bf16[1024,896]{1,0:T(8,128)(2,1)S(1)} %copy-done, bf16[896,256]{1,0:T(8,128)(2,1)S(1)} %copy-done.8, bf16[896,256]{1,0:T(8,128)(2,1)S(1)} %collective-permute-done.other_ref), custom_call_target="tpu_custom_call" | custom-call | flops 939524096 | bytes 3670016 | tf_op jit(solution)/shard_map/pallas_call | solution.py:147
  62.6 0.0 all-to-all-done.1.grad_ref
  62.6 0.0 copy-start.2
  62.6 2.6 %shard_map.79 = (bf16[8,128,896]{2,1,0:T(8,128)(2,1)}, f32[128,896]{1,0:T(8,128)S(1)}) custom-call(bf16[4,8,128,128]{3,2,1,0:T(8,128)(2,1)S(1)} %all-to-all-done.1.grad_ref, bf16[896,256]{1,0:T(8,128)(2,1)S(1)} %copy-done.8, bf16[896,256]{1,0:T(8,128)(2,1)S(1)} %collective-permute-done.other_ref), custom_call_target="tpu_custom_call" | custom-call | flops 939524096 | bytes 3670016 | tf_op jit(solution)/shard_map/pallas_call | solution.py:152
  65.2 0.0 copy-start.1
  65.2 0.0 reduce-scatter.2.cloned.1.call-update
  65.3 0.0 copy-done.2
  65.3 4.9 %all-to-all-start.2 = ((bf16[4,8,128,128]{3,2,1,0:T(8,128)(2,1)}), bf16[4,8,128,128]{3,2,1,0:T(8,128)(2,1)S(1)}, u32[]{:S(2)}, u32[]{:S(2)}) async-start(bf16[4,8,128,128]{3,2,1,0:T(8,128)(2,1)} %shard_map.76), calls=%async_computation.2 | async-start | bytes 2097152 | tf_op jit(solution)/shard_map/all_to_all | solution.py:132
  70.2 0.0 copy-done.1
  70.2 0.0 copy-start.3
  70.2 1.2 %copy-done.3 = bf16[4,8,128,128]{3,2,1,0:T(8,128)(2,1)S(1)} copy-done((bf16[4,8,128,128]{3,2,1,0:T(8,128)(2,1)S(1)}, bf16[4,8,128,128]{3,2,1,0:T(8,128)(2,1)}, u32[]{:S(2)}) %copy-start.3) | copy-done | bytes 1048600
  71.4 2.1 %shard_map.81 = (f32[896,256]{1,0:T(8,128)S(1)}, f32[896,256]{1,0:T(8,128)}) custom-call(bf16[1024,896]{1,0:T(8,128)(2,1)S(1)} %copy-done.1, bf16[4,8,128,128]{3,2,1,0:T(8,128)(2,1)S(1)} %copy-done.3), custom_call_target="tpu_custom_call" | custom-call | flops 939524096 | bytes 3670016 | tf_op jit(solution)/shard_map/pallas_call | solution.py:167
  73.6 0.0 copy-start.4
  73.6 0.9 copy-done.4
  74.5 0.0 copy-start.5
  74.5 2.0 %collective-permute-start.3 = (f32[896,256]{1,0:T(8,128)}, f32[896,256]{1,0:T(8,128)S(1)}, u32[]{:S(2)}, u32[]{:S(2)}) collective-permute-start(f32[896,256]{1,0:T(8,128)} %get-tuple-element.29), channel_id=1, source_target_pairs={{0,1},{1,0},{2,3},{3,2},{4,5},{5,4},{6,7},{7,6},{8,9},{9,8},{10,11... | collective-permute-start | bytes 2752520 | tf_op jit(solution)/shard_map/ppermute | solution.py:171
  76.5 1.6 %all-to-all-done.2.parts_ref = bf16[4,8,128,128]{3,2,1,0:T(8,128)(2,1)S(1)} async-done(((bf16[4,8,128,128]{3,2,1,0:T(8,128)(2,1)}), bf16[4,8,128,128]{3,2,1,0:T(8,128)(2,1)S(1)}, u32[]{:S(2)}, u32[]{:S(2)}) %all-to-all-start.2) | async-done | bytes 1048608 | tf_op jit(solution)/shard_map/all_to_all | solution.py:132
  78.1 0.1 shard_map.77
  78.3 0.0 copy-start.6
  78.3 0.0 copy-start.7
  78.3 12.7 %all_to_all.21.parts_ref = bf16[8,128,128]{2,1,0:T(8,128)(2,1)S(1)} all-to-all(bf16[8,128,128]{2,1,0:T(8,128)(2,1)S(1)} %shard_map.77), channel_id=1, replica_groups=mesh['x'=4,'y'=8,'z'=8,'core'=2] {'y'}, dimensions={0} | all-to-all | bytes 524288 | tf_op jit(solution)/shard_map/all_to_all | solution.py:132
  91.1 9.1 %collective-permute-start.2 = (bf16[128,128]{1,0:T(8,128)(2,1)S(1)}, bf16[128,128]{1,0:T(8,128)(2,1)S(1)}, u32[]{:S(2)}, u32[]{:S(2)}) collective-permute-start(bf16[128,128]{1,0:T(8,128)(2,1)S(1)} %shard_map.78), channel_id=1, source_target_pairs={{0,0},{257,1},{16,2},{273,3},{32,4},{289,5},{48,6},{305,7},{64,8},... | collective-permute-start | bytes 98312 | tf_op jit(solution)/shard_map/ppermute | solution.py:164
  100.2 0.0 collective-permute-done.3.b_ref
  100.2 0.0 copy-done.5
  100.2 0.8 shard_map.82
  101.1 9.2 %reduce-scatter.2.cloned.1.call-done.others_ref = bf16[128,896]{1,0:T(8,128)(2,1)} async-done(((bf16[1024,896]{1,0:T(8,128)(2,1)}), bf16[128,896]{1,0:T(8,128)(2,1)}) %reduce-scatter.2.cloned.1.call-update) | async-done | bytes 229392 | tf_op jit(solution)/shard_map/reduce_scatter | solution.py:155
  110.3 0.0 copy-done.6
  110.3 0.0 copy-done.7
  110.3 0.0 copy-start.9
  110.3 0.9 copy-done.9
  111.2 1.0 shard_map.80
  112.2 0.0 collective-permute-done.2
  112.2 0.6 copy.9
  (2 shorter events, 0.1 us)
Async XLA Ops:
  7.2 51.7 %all-gather.2.cloned.1.call-start = ((), (), s32[]{:S(2)}) async-start(), calls=%async_computation.5 | async-start | bytes 2064384 | tf_op jit(solution)/shard_map/all_gather | solution.py:140
  9.1 16.1 %collective-permute-start.1 = (bf16[128,128]{1,0:T(8,128)(2,1)}, bf16[128,128]{1,0:T(8,128)(2,1)S(1)}, u32[]{:S(2)}, u32[]{:S(2)}) collective-permute-start(bf16[128,128]{1,0:T(8,128)(2,1)} %param.7), channel_id=1, source_target_pairs={{0,0},{1,257},{2,16},{3,273},{4,32},{5,289},{6,48},{7,305},{8,64},... | collective-permute-start | bytes 98312 | tf_op jit(solution)/shard_map/ppermute | solution.py:142
  25.2 19.6 %copy-start.8 = (bf16[896,256]{1,0:T(8,128)(2,1)S(1)}, bf16[896,256]{1,0:T(8,128)(2,1)}, u32[]{:S(2)}) copy-start(bf16[896,256]{1,0:T(8,128)(2,1)} %own_ref.3) | copy-start | bytes 1376260
  40.0 22.6 %all-to-all-start.1 = ((bf16[4,8,128,128]{3,2,1,0:T(8,128)(2,1)}), bf16[4,8,128,128]{3,2,1,0:T(8,128)(2,1)S(1)}, u32[]{:S(2)}, u32[]{:S(2)}) async-start(bf16[4,8,128,128]{3,2,1,0:T(8,128)(2,1)} %broadcast_in_dim.7), calls=%async_computation.1 | async-start | bytes 2097152 | tf_op jit(solution)/shard_map/all_to_all | solution.py:132
  44.8 65.5 %reduce-scatter.2.cloned.1.call-start = ((), (), s32[]{:S(2)}) async-start(), calls=%async_computation.6 | async-start | bytes 2064384 | tf_op jit(solution)/shard_map/reduce_scatter | solution.py:155
  44.8 3.7 %collective-permute-start = (bf16[896,256]{1,0:T(8,128)(2,1)S(1)}, bf16[896,256]{1,0:T(8,128)(2,1)S(1)}, u32[]{:S(2)}, u32[]{:S(2)}) collective-permute-start(bf16[896,256]{1,0:T(8,128)(2,1)S(1)} %copy-done.8), channel_id=1, source_target_pairs={{0,1},{1,0},{2,3},{3,2},{4,5},{5,4},{6,7},{7,6},{8,9},{9,8},{10,11... | collective-permute-start | bytes 1376264 | tf_op jit(solution)/shard_map/ppermute | solution.py:143
  58.9 1.5 %copy-start = (bf16[1024,896]{1,0:T(8,128)(2,1)S(1)}, bf16[1024,896]{1,0:T(8,128)(2,1)}, u32[]{:S(2)}) copy-start(bf16[1024,896]{1,0:T(8,128)(2,1)} %all-gather.2.cloned.1.call-done.hidden_ref) | copy-start | bytes 5505028
  62.6 2.7 %copy-start.2 = (bf16[4,8,128,128]{3,2,1,0:T(8,128)(2,1)}, bf16[4,8,128,128]{3,2,1,0:T(8,128)(2,1)S(1)}, u32[]{:S(2)}) copy-start(bf16[4,8,128,128]{3,2,1,0:T(8,128)(2,1)S(1)} %all-to-all-done.1.grad_ref) | copy-start | bytes 3145732
  65.2 5.0 %copy-start.1 = (bf16[1024,896]{1,0:T(8,128)(2,1)S(1)}, bf16[1024,896]{1,0:T(8,128)(2,1)}, u32[]{:S(2)}) copy-start(bf16[1024,896]{1,0:T(8,128)(2,1)} %all-gather.2.cloned.1.call-done.hidden_ref) | copy-start | bytes 5505028
  65.3 12.9 %all-to-all-start.2 = ((bf16[4,8,128,128]{3,2,1,0:T(8,128)(2,1)}), bf16[4,8,128,128]{3,2,1,0:T(8,128)(2,1)S(1)}, u32[]{:S(2)}, u32[]{:S(2)}) async-start(bf16[4,8,128,128]{3,2,1,0:T(8,128)(2,1)} %shard_map.76), calls=%async_computation.2 | async-start | bytes 2097152 | tf_op jit(solution)/shard_map/all_to_all | solution.py:132
  70.2 1.2 %copy-start.3 = (bf16[4,8,128,128]{3,2,1,0:T(8,128)(2,1)S(1)}, bf16[4,8,128,128]{3,2,1,0:T(8,128)(2,1)}, u32[]{:S(2)}) copy-start(bf16[4,8,128,128]{3,2,1,0:T(8,128)(2,1)} %copy-done.2) | copy-start | bytes 3145732
  73.6 0.9 copy-start.4
  74.5 25.7 %copy-start.5 = (f32[896,256]{1,0:T(8,128)S(1)}, f32[896,256]{1,0:T(8,128)}, u32[]{:S(2)}) copy-start(f32[896,256]{1,0:T(8,128)} %copy-done.4) | copy-start | bytes 2752516
  74.5 25.7 %collective-permute-start.3 = (f32[896,256]{1,0:T(8,128)}, f32[896,256]{1,0:T(8,128)S(1)}, u32[]{:S(2)}, u32[]{:S(2)}) collective-permute-start(f32[896,256]{1,0:T(8,128)} %get-tuple-element.29), channel_id=1, source_target_pairs={{0,1},{1,0},{2,3},{3,2},{4,5},{5,4},{6,7},{7,6},{8,9},{9,8},{10,11... | collective-permute-start | bytes 2752520 | tf_op jit(solution)/shard_map/ppermute | solution.py:171
  78.3 32.0 %copy-start.6 = (bf16[128,896]{1,0:T(8,128)(2,1)S(1)}, bf16[128,896]{1,0:T(8,128)(2,1)}, u32[]{:S(2)}) copy-start(bf16[128,896]{1,0:T(8,128)(2,1)} %gate_ref.3) | copy-start | bytes 688132
  78.3 32.0 %copy-start.7 = (bf16[128,896]{1,0:T(8,128)(2,1)S(1)}, bf16[128,896]{1,0:T(8,128)(2,1)}, u32[]{:S(2)}) copy-start(bf16[128,896]{1,0:T(8,128)(2,1)} %up_ref.3) | copy-start | bytes 688132
  91.1 21.1 %collective-permute-start.2 = (bf16[128,128]{1,0:T(8,128)(2,1)S(1)}, bf16[128,128]{1,0:T(8,128)(2,1)S(1)}, u32[]{:S(2)}, u32[]{:S(2)}) collective-permute-start(bf16[128,128]{1,0:T(8,128)(2,1)S(1)} %shard_map.78), channel_id=1, source_target_pairs={{0,0},{257,1},{16,2},{273,3},{32,4},{289,5},{48,6},{305,7},{64,8},... | collective-permute-start | bytes 98312 | tf_op jit(solution)/shard_map/ppermute | solution.py:164
  110.3 0.9 copy-start.9
Sparse Core Ops, SparseCore 0:
  10.7 48.1 all-gather.1
  65.4 44.8 reduce-scatter.1

commit v3 on v2

--- a/solution.py
+++ b/solution.py
@@ -1,25 +1,49 @@
 import jax
 import jax.numpy as jnp
+import numpy as np
 from jax import lax
 from jax.experimental import pallas as pl
 from jax.experimental.pallas import tpu as pltpu
 from jax.sharding import Mesh, PartitionSpec as P
 
 X, Y, Z, CORES = 4, 8, 8, 2
-AXES = ("x", "y", "z", "core")
+SIDES = 2
+AXES = ("x", "step", "side", "z", "core")
+
+
 def index_of(x, y, z, core):
     return ((x * Y + y) * Z + z) * CORES + core
 
 
+def place(z, tokens, q):
+    ahead = lax.rem(tokens - z + Z, Z)
+    even = lax.rem(ahead, 2) == 0
+    turn = jnp.where(ahead >= 4, jnp.where(even, 0, 3), jnp.where(even, 2, 1))
+    first = 4 * lax.rem(z, 2)
+    y = jnp.where((ahead < 2) | (ahead > 5), lax.rem(first + 7 - q, Y), first + q)
+    return lax.rem(z // 2 + turn, X), y
+
+
 def to_feature_owner():
-    pairs = []
-    for x in range(X):
-        for y in range(Y):
-            for z in range(Z):
-                for core in range(CORES):
-                    target = index_of((y % 4 + 2 * core) % 4, z, 2 * x + y // 4, core)
-                    pairs.append((index_of(x, y, z, core), target))
-    return pairs
+    x, y, z, core = (a.ravel() for a in np.indices((X, Y, Z, CORES)))
+    plane = 2 * x + y // 4
+    ahead = (z - plane) % Z
+    turn = np.array([2, 1, 2, 1, 0, 3, 0, 3])[ahead]
+    target_y = np.where((ahead < 2) | (ahead > 5), (4 * (plane % 2) + 7 - y % 4) % Y, y)
+    targets = index_of((plane // 2 + turn) % X, target_y, plane, core)
+    return [(int(a), int(b)) for a, b in zip(index_of(x, y, z, core), targets)]
+
+
+def slot(tokens, half, h):
+    core = lax.axis_index("core")
+    q = 2 * (core if half == 0 else 1 - core) + h
+    x, y = place(lax.axis_index("z"), tokens, q)
+    return x * SIDES + lax.rem(y, SIDES), y // SIDES
+
+
+def grad_of(grad_ref, tokens, half):
+    blocks = [jnp.concatenate([grad_ref[slot(t, half, h)] for h in range(2)], axis=1) for t in tokens]
+    return jnp.concatenate(blocks, axis=0)
 
 
 def kernel_call(kernel, out_shape, flops, size, vmem=24, **more):
@@ -67,33 +91,34 @@
 
 
 def share_kernel(grad_ref, own_ref, other_ref, share_ref, mine_ref):
-    z_blocks, tokens, _ = share_ref.shape
     weights = jnp.concatenate([own_ref[...], other_ref[...]], axis=1)
 
-    def product(grad):
+    def product(tokens):
+        grad = jnp.concatenate([grad_of(grad_ref, tokens, half) for half in range(2)], axis=1)
         return lax.dot_general(grad, weights, (((1,), (1,)), ((), ())), preferred_element_type=jnp.float32)
 
-    grad = jnp.concatenate([grad_ref[q].reshape(z_blocks * tokens, -1) for q in range(X)], axis=1)
-    share_ref[...] = product(grad).astype(jnp.bfloat16).reshape(share_ref.shape)
+    share_ref[...] = product(range(Z)).astype(jnp.bfloat16).reshape(share_ref.shape)
     here = lax.axis_index("z")
     share_ref[here] = jnp.zeros(mine_ref.shape, jnp.bfloat16)
-    mine_ref[...] = product(jnp.concatenate([grad_ref[q, here] for q in range(X)], axis=1))
+    mine_ref[...] = product([here])
 
 
 def output_kernel(hidden_ref, own_ref, other_ref, out_ref):
-    _, z_blocks, tokens, sub = out_ref.shape
+    _, _, tokens, sub = out_ref.shape
     for half, weights in enumerate((own_ref, other_ref)):
         product = jnp.dot(hidden_ref[...], weights[...], preferred_element_type=jnp.float32).astype(jnp.bfloat16)
-        for h in range(2):
-            out_ref[2 * half + h] = product[:, h * sub : (h + 1) * sub].reshape(z_blocks, tokens, sub)
+        for z in range(Z):
+            for h in range(2):
+                out_ref[slot(z, half, h)] = product[z * tokens : (z + 1) * tokens, h * sub : (h + 1) * sub]
 
 
 def weight_grad_kernel(hidden_ref, grad_ref, own_ref, other_ref):
-    rows = hidden_ref.shape[0]
     for half, out_ref in enumerate((own_ref, other_ref)):
-        grad = jnp.concatenate([grad_ref[2 * half + h].reshape(rows, -1) for h in range(2)], axis=1)
         out_ref[...] = lax.dot_general(
-            hidden_ref[...], grad, (((0,), (0,)), ((), ())), preferred_element_type=jnp.float32
+            hidden_ref[...],
+            grad_of(grad_ref, range(Z), half),
+            (((0,), (0,)), ((), ())),
+            preferred_element_type=jnp.float32,
         ).astype(out_ref.dtype)
 
 
@@ -141,26 +166,27 @@
 
     grad = lax.ppermute(out_grad, AXES, there)
     other_weight = lax.ppermute(down_weight, "core", swap)
-    grad = exchanged(jnp.broadcast_to(grad, (Y, tokens, sub)), "y")
-    grad = exchanged(jnp.broadcast_to(grad, (X, Y, tokens, sub)), "x")
-
-    output = kernel_call(output_kernel, shape((X, Y, tokens, sub), bf16), flops, 4 * rows * units)(
-        hidden_all, down_weight, other_weight
-    )
-    output, grad = together((output, grad))
+    steps = Y // SIDES
+    grad = exchanged(jnp.broadcast_to(grad, (steps, tokens, sub)), "step")
+    grad = exchanged(jnp.broadcast_to(grad, (X * SIDES, steps, tokens, sub)), ("x", "side"))
 
     share, mine = kernel_call(
         share_kernel, (shape((Z, tokens, units), bf16), shape(block, f32)), flops, 4 * rows * units
     )(grad, down_weight, other_weight)
+    hidden_all, share = together((hidden_all, share))
+    output = kernel_call(output_kernel, shape((X * SIDES, steps, tokens, sub), bf16), flops, 4 * rows * units)(
+        hidden_all, down_weight, other_weight
+    )
+
     others = lax.psum_scatter(share.reshape(rows, units), "z", scatter_dimension=0, tiled=True)
     gate_grad, up_grad = kernel_call(gradient_kernel, (shape(block, bf16),) * 2, 0, 14 * tokens * units)(
         mine, others, gate_pre, up_pre
     )
 
-    output = exchanged(output, "x")
-    output = kernel_call(sum_kernel, shape((Y, tokens, sub), bf16), 0, 10 * rows * sub)(output)
-    output = exchanged(output, "y")
-    output = kernel_call(sum_kernel, shape((tokens, sub), bf16), 0, 18 * tokens * sub)(output)
+    output = exchanged(output, ("x", "side"))
+    output = kernel_call(sum_kernel, shape((steps, tokens, sub), bf16), 0, 10 * rows * sub)(output)
+    output = exchanged(output, "step")
+    output = kernel_call(sum_kernel, shape((tokens, sub), bf16), 0, 10 * tokens * sub)(output)
     output = lax.ppermute(output, AXES, back)
     output, gate_grad, up_grad = together((output, gate_grad, up_grad))
 
@@ -174,9 +200,9 @@
 
 
 def solution(mesh):
-    chips = Mesh(mesh.devices.reshape(X, Y, Z, CORES), AXES)
-    by_token = P(("z", "core"), ("x", "y"))
-    by_unit = P(("x", "y"), ("z", "core"))
+    chips = Mesh(mesh.devices.reshape(X, Y // SIDES, SIDES, Z, CORES), AXES)
+    by_token = P(("z", "core"), ("x", "step", "side"))
+    by_unit = P(("x", "step", "side"), ("z", "core"))
     return jax.shard_map(
         body,
         mesh=chips,

time: 120 us -> 116 us (0.967)
  the two profiles are of different devices: /device:TPU:36 before, /device:TPU:16 now
where the time goes in v3:
time: 116 us; the launch traced here: 115 us
  starting transfers between devices  29.4 us (25%)
  blocking collectives  26.8 us (23%)
  waiting for transfers between devices  25.6 us (22%)
  between operations  14.2 us (12%)
  Pallas kernels  10.9 us (9%)
  local copies, waits for them, and re-layouts  8.23 us (7%)
    all_to_all x2, blocking collectives, exchanged(): return lax.all_to_all(array, axis, split_axis=0, concat_axis=0, tiled=True)  26.8 us
    all_to_all x2, waiting for transfers between devices, exchanged(): return lax.all_to_all(array, axis, split_axis=0, concat_axis=0, tiled=True)  15.6 us
    all_to_all x2, starting transfers between devices, exchanged(): return lax.all_to_all(array, axis, split_axis=0, concat_axis=0, tiled=True)  9.75 us
    ppermute x1, starting transfers between devices, body(): grad = lax.ppermute(out_grad, AXES, there)  8.42 us
    ppermute x1, starting transfers between devices, body(): output = lax.ppermute(output, AXES, back)  7.25 us
    unnamed x27, local copies, waits for them, and re-layouts  6.96 us
    ppermute x1, waiting for transfers between devices, body(): grad = lax.ppermute(out_grad, AXES, there)  4.76 us
    reduce_scatter x1, waiting for transfers between devices, body(): lax.psum_scatter(share.reshape(rows, units), 'z', scatter_dimension=0, ti...  3.47 us
  transfers between devices with their start and end apart: 8, of which 5 were waited for; matrix products, arithmetic and copies ran while one was open for 1% of the time, Pallas kernels for 8%

profile of v3, /device:TPU:16, one launch (start us, length us, event | category | flops | bytes accessed | tf_op | source)
XLA Modules:
  0.0 115.1 jit_solution(1610752396282539373)
XLA Ops:
  7.2 0.0 all-gather.2.cloned.1.call-start
  7.2 1.9 %shard_map.75 = bf16[128,896]{1,0:T(8,128)(2,1)} custom-call(bf16[128,896]{1,0:T(8,128)(2,1)} %gate_ref.3, bf16[128,896]{1,0:T(8,128)(2,1)} %up_ref.3), custom_call_target="tpu_custom_call" | custom-call | bytes 688128 | tf_op jit(solution)/shard_map/pallas_call | solution.py:63
  9.1 0.0 all-gather.2.cloned.1.call-update
  9.1 0.0 copy-start.9
  9.1 8.4 %collective-permute-start = (bf16[128,128]{1,0:T(8,128)(2,1)}, bf16[128,128]{1,0:T(8,128)(2,1)S(1)}, u32[]{:S(2)}, u32[]{:S(2)}) collective-permute-start(bf16[128,128]{1,0:T(8,128)(2,1)} %param.7), channel_id=1, source_target_pairs={{0,368},{1,369},{2,240},{3,241},{4,256},{5,257},{6,128},{7,129},{8... | collective-permute-start | bytes 98312 | tf_op jit(solution)/shard_map/ppermute | solution.py:167
  17.5 4.8 %collective-permute-done = bf16[128,128]{1,0:T(8,128)(2,1)S(1)} collective-permute-done((bf16[128,128]{1,0:T(8,128)(2,1)}, bf16[128,128]{1,0:T(8,128)(2,1)S(1)}, u32[]{:S(2)}, u32[]{:S(2)}) %collective-permute-start) | collective-permute-done | bytes 32800 | tf_op jit(solution)/shard_map/ppermute | solution.py:167
  22.3 14.1 %all_to_all.20 = bf16[4,128,128]{2,1,0:T(8,128)(2,1)S(1)} all-to-all(bf16[4,128,128]{2,1,0:T(8,128)(2,1)S(1)} %broadcast_in_dim.6), channel_id=1, replica_groups=mesh['x'=4,'step'=4,'side'=2,'z'=8,'core'=2] {'step'}, dimensions={0} | all-to-all | bytes 262144 | tf_op jit(solution)/shard_map/all_to_all | solution.py:157
  36.4 1.2 %broadcast_in_dim.7 = bf16[8,4,128,128]{3,2,1,0:T(8,128)(2,1)} broadcast(bf16[4,128,128]{2,1,0:T(8,128)(2,1)S(1)} %all_to_all.20), dimensions={1,2,3} | broadcast | bytes 1179648 | tf_op jit(solution)/shard_map/broadcast_in_dim | solution.py:171
  37.7 4.6 %all-to-all-start.1 = ((bf16[8,4,128,128]{3,2,1,0:T(8,128)(2,1)}), bf16[8,4,128,128]{3,2,1,0:T(8,128)(2,1)S(1)}, u32[]{:S(2)}, u32[]{:S(2)}) async-start(bf16[8,4,128,128]{3,2,1,0:T(8,128)(2,1)} %broadcast_in_dim.7), calls=%async_computation.1 | async-start | bytes 2097152 | tf_op jit(solution)/shard_map/all_to_all | solution.py:157
  42.3 0.0 reduce-scatter.2.cloned.1.call-start
  42.4 0.0 copy-done.9
  42.4 1.9 %collective-permute-start.1 = (bf16[896,256]{1,0:T(8,128)(2,1)S(1)}, bf16[896,256]{1,0:T(8,128)(2,1)S(1)}, u32[]{:S(2)}, u32[]{:S(2)}) collective-permute-start(bf16[896,256]{1,0:T(8,128)(2,1)S(1)} %copy-done.9), channel_id=1, source_target_pairs={{0,1},{1,0},{2,3},{3,2},{4,5},{5,4},{6,7},{7,6},{8,9},{9,8},{10,11... | collective-permute-start | bytes 1376264 | tf_op jit(solution)/shard_map/ppermute | solution.py:168
  44.3 1.8 %collective-permute-done.1.other_ref = bf16[896,256]{1,0:T(8,128)(2,1)S(1)} collective-permute-done((bf16[896,256]{1,0:T(8,128)(2,1)S(1)}, bf16[896,256]{1,0:T(8,128)(2,1)S(1)}, u32[]{:S(2)}, u32[]{:S(2)}) %collective-permute-start.1) | collective-permute-done | bytes 458784 | tf_op jit(solution)/shard_map/ppermute | solution.py:168
  46.1 0.0 copy-start.10
  46.1 9.6 %all-to-all-done.1.grad_ref = bf16[8,4,128,128]{3,2,1,0:T(8,128)(2,1)S(1)} async-done(((bf16[8,4,128,128]{3,2,1,0:T(8,128)(2,1)}), bf16[8,4,128,128]{3,2,1,0:T(8,128)(2,1)S(1)}, u32[]{:S(2)}, u32[]{:S(2)}) %all-to-all-start.1) | async-done | bytes 1048608 | tf_op jit(solution)/shard_map/all_to_all | solution.py:157
  55.7 0.0 copy-start.1
  55.8 2.6 %shard_map.76 = (bf16[8,128,896]{2,1,0:T(8,128)(2,1)}, f32[128,896]{1,0:T(8,128)S(1)}) custom-call(bf16[8,4,128,128]{3,2,1,0:T(8,128)(2,1)S(1)} %all-to-all-done.1.grad_ref, bf16[896,256]{1,0:T(8,128)(2,1)S(1)} %copy-done.9, bf16[896,256]{1,0:T(8,128)(2,1)S(1)} %collective-permute-done.1.other_ref), custom_call_target="tpu_custom_call" | custom-call | flops 939524096 | bytes 3670016 | tf_op jit(solution)/shard_map/pallas_call | solution.py:173
  58.4 0.0 copy-done.10
  58.4 0.0 copy-start.7
  58.4 0.8 copy-done.7
  59.1 0.0 all-gather.2.cloned.1.call-done.hidden_ref
  59.1 0.0 copy-start
  59.2 0.0 reduce-scatter.2.cloned.1.call-update
  59.2 0.0 copy-done.1
  59.2 1.5 %copy-done = bf16[1024,896]{1,0:T(8,128)(2,1)S(1)} copy-done((bf16[1024,896]{1,0:T(8,128)(2,1)S(1)}, bf16[1024,896]{1,0:T(8,128)(2,1)}, u32[]{:S(2)}) %copy-start) | copy-done | bytes 1835032
  60.7 0.0 copy-start.11
  60.7 1.0 copy-done.11
  61.7 2.3 %shard_map.77 = bf16[8,4,128,128]{3,2,1,0:T(8,128)(2,1)} custom-call(bf16[1024,896]{1,0:T(8,128)(2,1)S(1)} %copy-done, bf16[896,256]{1,0:T(8,128)(2,1)S(1)} %copy-done.9, bf16[896,256]{1,0:T(8,128)(2,1)S(1)} %copy-done.11), custom_call_target="tpu_custom_call" | custom-call | flops 939524096 | bytes 3670016 | tf_op jit(solution)/shard_map/pallas_call | solution.py:177
  64.0 5.1 %all-to-all-start.2 = ((bf16[8,4,128,128]{3,2,1,0:T(8,128)(2,1)}), bf16[8,4,128,128]{3,2,1,0:T(8,128)(2,1)S(1)}, u32[]{:S(2)}, u32[]{:S(2)}) async-start(bf16[8,4,128,128]{3,2,1,0:T(8,128)(2,1)} %shard_map.77), calls=%async_computation.2 | async-start | bytes 2097152 | tf_op jit(solution)/shard_map/all_to_all | solution.py:157
  69.1 0.0 copy-start.2
  69.1 1.2 %copy-done.2 = bf16[8,4,128,128]{3,2,1,0:T(8,128)(2,1)S(1)} copy-done((bf16[8,4,128,128]{3,2,1,0:T(8,128)(2,1)S(1)}, bf16[8,4,128,128]{3,2,1,0:T(8,128)(2,1)}, u32[]{:S(2)}) %copy-start.2) | copy-done | bytes 1048600
  70.3 2.2 %shard_map.81 = (f32[896,256]{1,0:T(8,128)S(1)}, f32[896,256]{1,0:T(8,128)}) custom-call(bf16[1024,896]{1,0:T(8,128)(2,1)S(1)} %copy-done, bf16[8,4,128,128]{3,2,1,0:T(8,128)(2,1)S(1)} %copy-done.2), custom_call_target="tpu_custom_call" | custom-call | flops 939524096 | bytes 3670016 | tf_op jit(solution)/shard_map/pallas_call | solution.py:193
  72.4 0.0 copy-start.3
  72.4 0.9 copy-done.3
  73.4 0.0 copy-start.4
  73.4 0.0 copy-start.5
  73.4 0.0 copy-start.6
  73.4 2.0 %collective-permute-start.3 = (f32[896,256]{1,0:T(8,128)}, f32[896,256]{1,0:T(8,128)S(1)}, u32[]{:S(2)}, u32[]{:S(2)}) collective-permute-start(f32[896,256]{1,0:T(8,128)} %get-tuple-element.29), channel_id=1, source_target_pairs={{0,1},{1,0},{2,3},{3,2},{4,5},{5,4},{6,7},{7,6},{8,9},{9,8},{10,11... | collective-permute-start | bytes 2752520 | tf_op jit(solution)/shard_map/ppermute | solution.py:197
  75.4 5.9 %all-to-all-done.2.parts_ref = bf16[8,4,128,128]{3,2,1,0:T(8,128)(2,1)S(1)} async-done(((bf16[8,4,128,128]{3,2,1,0:T(8,128)(2,1)}), bf16[8,4,128,128]{3,2,1,0:T(8,128)(2,1)S(1)}, u32[]{:S(2)}, u32[]{:S(2)}) %all-to-all-start.2) | async-done | bytes 1048608 | tf_op jit(solution)/shard_map/all_to_all | solution.py:157
  81.4 0.1 shard_map.78
  81.5 0.0 copy-start.8
  81.5 12.6 %all_to_all.21.parts_ref = bf16[4,128,128]{2,1,0:T(8,128)(2,1)S(1)} all-to-all(bf16[4,128,128]{2,1,0:T(8,128)(2,1)S(1)} %shard_map.78), channel_id=1, replica_groups=mesh['x'=4,'step'=4,'side'=2,'z'=8,'core'=2] {'step'}, dimensions={0} | all-to-all | bytes 262144 | tf_op jit(solution)/shard_map/all_to_all | solution.py:157
  94.2 7.2 %collective-permute-start.2 = (bf16[128,128]{1,0:T(8,128)(2,1)S(1)}, bf16[128,128]{1,0:T(8,128)(2,1)S(1)}, u32[]{:S(2)}, u32[]{:S(2)}) collective-permute-start(bf16[128,128]{1,0:T(8,128)(2,1)S(1)} %shard_map.79), channel_id=1, source_target_pairs={{368,0},{369,1},{240,2},{241,3},{256,4},{257,5},{128,6},{129,7},{0... | collective-permute-start | bytes 98312 | tf_op jit(solution)/shard_map/ppermute | solution.py:190
  101.4 0.0 collective-permute-done.3.b_ref
  101.4 0.0 copy-done.4
  101.4 0.8 shard_map.82
  102.3 3.5 %reduce-scatter.2.cloned.1.call-done.others_ref = bf16[128,896]{1,0:T(8,128)(2,1)} async-done(((bf16[1024,896]{1,0:T(8,128)(2,1)}), bf16[128,896]{1,0:T(8,128)(2,1)}) %reduce-scatter.2.cloned.1.call-update) | async-done | bytes 229392 | tf_op jit(solution)/shard_map/reduce_scatter | solution.py:181
  105.8 0.0 copy-done.5
  105.8 0.0 copy-done.6
  105.8 0.0 copy-done.8
  105.8 0.0 copy-start.12
  105.8 0.9 copy-done.12
  106.7 1.0 shard_map.80
  107.7 0.0 collective-permute-done.2
  107.7 0.6 copy.9
  (2 shorter events, 0.0 us)
Async XLA Ops:
  7.2 52.0 %all-gather.2.cloned.1.call-start = ((), (), s32[]{:S(2)}) async-start(), calls=%async_computation.5 | async-start | bytes 2064384 | tf_op jit(solution)/shard_map/all_gather | solution.py:165
  9.1 33.3 %copy-start.9 = (bf16[896,256]{1,0:T(8,128)(2,1)S(1)}, bf16[896,256]{1,0:T(8,128)(2,1)}, u32[]{:S(2)}) copy-start(bf16[896,256]{1,0:T(8,128)(2,1)} %own_ref.3) | copy-start | bytes 1376260
  9.1 13.2 %collective-permute-start = (bf16[128,128]{1,0:T(8,128)(2,1)}, bf16[128,128]{1,0:T(8,128)(2,1)S(1)}, u32[]{:S(2)}, u32[]{:S(2)}) collective-permute-start(bf16[128,128]{1,0:T(8,128)(2,1)} %param.7), channel_id=1, source_target_pairs={{0,368},{1,369},{2,240},{3,241},{4,256},{5,257},{6,128},{7,129},{8... | collective-permute-start | bytes 98312 | tf_op jit(solution)/shard_map/ppermute | solution.py:167
  37.7 18.1 %all-to-all-start.1 = ((bf16[8,4,128,128]{3,2,1,0:T(8,128)(2,1)}), bf16[8,4,128,128]{3,2,1,0:T(8,128)(2,1)S(1)}, u32[]{:S(2)}, u32[]{:S(2)}) async-start(bf16[8,4,128,128]{3,2,1,0:T(8,128)(2,1)} %broadcast_in_dim.7), calls=%async_computation.1 | async-start | bytes 2097152 | tf_op jit(solution)/shard_map/all_to_all | solution.py:157
  42.3 63.4 %reduce-scatter.2.cloned.1.call-start = ((), (), s32[]{:S(2)}) async-start(), calls=%async_computation.6 | async-start | bytes 2064384 | tf_op jit(solution)/shard_map/reduce_scatter | solution.py:181
  42.4 3.7 %collective-permute-start.1 = (bf16[896,256]{1,0:T(8,128)(2,1)S(1)}, bf16[896,256]{1,0:T(8,128)(2,1)S(1)}, u32[]{:S(2)}, u32[]{:S(2)}) collective-permute-start(bf16[896,256]{1,0:T(8,128)(2,1)S(1)} %copy-done.9), channel_id=1, source_target_pairs={{0,1},{1,0},{2,3},{3,2},{4,5},{5,4},{6,7},{7,6},{8,9},{9,8},{10,11... | collective-permute-start | bytes 1376264 | tf_op jit(solution)/shard_map/ppermute | solution.py:168
  46.1 12.3 %copy-start.10 = (bf16[896,256]{1,0:T(8,128)(2,1)}, bf16[896,256]{1,0:T(8,128)(2,1)S(1)}, u32[]{:S(2)}) copy-start(bf16[896,256]{1,0:T(8,128)(2,1)S(1)} %collective-permute-done.1.other_ref) | copy-start | bytes 1376260
  55.7 3.4 %copy-start.1 = (bf16[8,4,128,128]{3,2,1,0:T(8,128)(2,1)}, bf16[8,4,128,128]{3,2,1,0:T(8,128)(2,1)S(1)}, u32[]{:S(2)}) copy-start(bf16[8,4,128,128]{3,2,1,0:T(8,128)(2,1)S(1)} %all-to-all-done.1.grad_ref) | copy-start | bytes 3145732
  58.4 0.8 copy-start.7
  59.1 1.5 %copy-start = (bf16[1024,896]{1,0:T(8,128)(2,1)S(1)}, bf16[1024,896]{1,0:T(8,128)(2,1)}, u32[]{:S(2)}) copy-start(bf16[1024,896]{1,0:T(8,128)(2,1)} %all-gather.2.cloned.1.call-done.hidden_ref) | copy-start | bytes 5505028
  60.7 1.0 copy-start.11
  64.0 17.4 %all-to-all-start.2 = ((bf16[8,4,128,128]{3,2,1,0:T(8,128)(2,1)}), bf16[8,4,128,128]{3,2,1,0:T(8,128)(2,1)S(1)}, u32[]{:S(2)}, u32[]{:S(2)}) async-start(bf16[8,4,128,128]{3,2,1,0:T(8,128)(2,1)} %shard_map.77), calls=%async_computation.2 | async-start | bytes 2097152 | tf_op jit(solution)/shard_map/all_to_all | solution.py:157
  69.1 1.2 %copy-start.2 = (bf16[8,4,128,128]{3,2,1,0:T(8,128)(2,1)S(1)}, bf16[8,4,128,128]{3,2,1,0:T(8,128)(2,1)}, u32[]{:S(2)}) copy-start(bf16[8,4,128,128]{3,2,1,0:T(8,128)(2,1)} %copy-done.1) | copy-start | bytes 3145732
  72.4 0.9 copy-start.3
  73.4 28.1 %copy-start.4 = (f32[896,256]{1,0:T(8,128)S(1)}, f32[896,256]{1,0:T(8,128)}, u32[]{:S(2)}) copy-start(f32[896,256]{1,0:T(8,128)} %copy-done.3) | copy-start | bytes 2752516
  73.4 32.4 %copy-start.5 = (bf16[128,896]{1,0:T(8,128)(2,1)S(1)}, bf16[128,896]{1,0:T(8,128)(2,1)}, u32[]{:S(2)}) copy-start(bf16[128,896]{1,0:T(8,128)(2,1)} %gate_ref.3) | copy-start | bytes 688132
  73.4 32.4 %copy-start.6 = (bf16[128,896]{1,0:T(8,128)(2,1)S(1)}, bf16[128,896]{1,0:T(8,128)(2,1)}, u32[]{:S(2)}) copy-start(bf16[128,896]{1,0:T(8,128)(2,1)} %up_ref.3) | copy-start | bytes 688132
  73.4 28.1 %collective-permute-start.3 = (f32[896,256]{1,0:T(8,128)}, f32[896,256]{1,0:T(8,128)S(1)}, u32[]{:S(2)}, u32[]{:S(2)}) collective-permute-start(f32[896,256]{1,0:T(8,128)} %get-tuple-element.29), channel_id=1, source_target_pairs={{0,1},{1,0},{2,3},{3,2},{4,5},{5,4},{6,7},{7,6},{8,9},{9,8},{10,11... | collective-permute-start | bytes 2752520 | tf_op jit(solution)/shard_map/ppermute | solution.py:197
  81.5 24.3 %copy-start.8 = (f32[128,896]{1,0:T(8,128)S(1)}, f32[128,896]{1,0:T(8,128)}, u32[]{:S(2)}) copy-start(f32[128,896]{1,0:T(8,128)} %copy-done.7) | copy-start | bytes 1376260
  94.2 13.5 %collective-permute-start.2 = (bf16[128,128]{1,0:T(8,128)(2,1)S(1)}, bf16[128,128]{1,0:T(8,128)(2,1)S(1)}, u32[]{:S(2)}, u32[]{:S(2)}) collective-permute-start(bf16[128,128]{1,0:T(8,128)(2,1)S(1)} %shard_map.79), channel_id=1, source_target_pairs={{368,0},{369,1},{240,2},{241,3},{256,4},{257,5},{128,6},{129,7},{0... | collective-permute-start | bytes 98312 | tf_op jit(solution)/shard_map/ppermute | solution.py:190
  105.8 0.9 copy-start.12
Sparse Core Ops, SparseCore 0:
  10.7 48.3 all-gather.1
  61.9 43.7 reduce-scatter.1

commit v4 on v3

--- a/solution.py
+++ b/solution.py
@@ -81,13 +81,23 @@
 
 
 def hidden_kernel(gate_ref, up_ref, hidden_ref, gate_in, up_in, hidden_out, sems):
-    copies = [started(gate_ref, gate_in, sems.at[0]), started(up_ref, up_in, sems.at[1])]
-    for copy in copies:
-        copy.wait()
-    gate = gate_in[...].astype(jnp.float32)
-    up = up_in[...].astype(jnp.float32)
-    hidden_out[...] = (gate * jax.nn.sigmoid(gate) * up).astype(jnp.bfloat16)
-    started(hidden_out, hidden_ref, sems.at[2]).wait()
+    parts = 2
+    rows = gate_ref.shape[0] // parts
+    spans = [pl.ds(i * rows, rows) for i in range(parts)]
+    copies = [
+        (started(gate_ref.at[r], gate_in.at[r], sems.at[2 * i]), started(up_ref.at[r], up_in.at[r], sems.at[2 * i + 1]))
+        for i, r in enumerate(spans)
+    ]
+    stores = []
+    for i, r in enumerate(spans):
+        for copy in copies[i]:
+            copy.wait()
+        gate = gate_in[r].astype(jnp.float32)
+        up = up_in[r].astype(jnp.float32)
+        hidden_out[r] = (gate * jax.nn.sigmoid(gate) * up).astype(jnp.bfloat16)
+        stores.append(started(hidden_out.at[r], hidden_ref.at[r], sems.at[2 * parts + i]))
+    for store in stores:
+        store.wait()
 
 
 def share_kernel(grad_ref, own_ref, other_ref, share_ref, mine_ref):
@@ -159,7 +169,7 @@
     block = (tokens, units)
     vmem, dma = pltpu.VMEM, pltpu.SemaphoreType.DMA
     hidden = streamed_call(
-        hidden_kernel, shape(block, bf16), 0, 6 * tokens * units, [vmem(block, bf16)] * 3 + [dma((3,))]
+        hidden_kernel, shape(block, bf16), 0, 6 * tokens * units, [vmem(block, bf16)] * 3 + [dma((6,))]
     )(gate_pre, up_pre)
     hidden, out_grad = together((hidden, out_grad))
     hidden_all = lax.all_gather(hidden, "z", axis=0, tiled=True)
@@ -173,7 +183,7 @@
     share, mine = kernel_call(
         share_kernel, (shape((Z, tokens, units), bf16), shape(block, f32)), flops, 4 * rows * units
     )(grad, down_weight, other_weight)
-    hidden_all, share = together((hidden_all, share))
+    hidden_all, _ = together((hidden_all, mine))
     output = kernel_call(output_kernel, shape((X * SIDES, steps, tokens, sub), bf16), flops, 4 * rows * units)(
         hidden_all, down_weight, other_weight
     )

time: 116 us -> 115 us (level)
    unnamed x27 -> x25, local copies, waits for them, and re-layouts: 6.96 us -> 6.01 us
where the time goes in v4:
time: 115 us
  starting transfers between devices  29.6 us (26%)
  blocking collectives  26.8 us (23%)
  waiting for transfers between devices  26.2 us (23%)
  between operations  14.2 us (12%)
  Pallas kernels  10.9 us (9%)
  local copies, waits for them, and re-layouts  7.28 us (6%)
    all_to_all x2, blocking collectives, exchanged(): return lax.all_to_all(array, axis, split_axis=0, concat_axis=0, tiled=True)  26.8 us
    all_to_all x2, waiting for transfers between devices, exchanged(): return lax.all_to_all(array, axis, split_axis=0, concat_axis=0, tiled=True)  15.6 us
    all_to_all x2, starting transfers between devices, exchanged(): return lax.all_to_all(array, axis, split_axis=0, concat_axis=0, tiled=True)  9.84 us
    ppermute x1, starting transfers between devices, body(): grad = lax.ppermute(out_grad, AXES, there)  8.42 us
    ppermute x1, starting transfers between devices, body(): output = lax.ppermute(output, AXES, back)  7.28 us
    unnamed x25, local copies, waits for them, and re-layouts  6.01 us
    ppermute x1, waiting for transfers between devices, body(): grad = lax.ppermute(out_grad, AXES, there)  4.76 us
    reduce_scatter x1, waiting for transfers between devices, body(): lax.psum_scatter(share.reshape(rows, units), 'z', scatter_dimension=0, ti...  4.03 us
  transfers between devices with their start and end apart: 8, of which 5 were waited for; matrix products, arithmetic and copies ran while one was open for 1% of the time, Pallas kernels for 8%

profile of v4, /device:TPU:16, one launch (start us, length us, event | category | flops | bytes accessed | tf_op | source)
XLA Modules:
  0.0 114.8 jit_solution(5935298402745991886)
XLA Ops:
  7.2 0.0 all-gather.2.cloned.1.call-start
  7.2 1.8 %shard_map.75 = bf16[128,896]{1,0:T(8,128)(2,1)} custom-call(bf16[128,896]{1,0:T(8,128)(2,1)} %gate_ref.3, bf16[128,896]{1,0:T(8,128)(2,1)} %up_ref.3), custom_call_target="tpu_custom_call" | custom-call | bytes 688128 | tf_op jit(solution)/shard_map/pallas_call | solution.py:63
  9.0 0.0 all-gather.2.cloned.1.call-update
  9.1 0.0 copy-start.10
  9.1 8.4 %collective-permute-start = (bf16[128,128]{1,0:T(8,128)(2,1)}, bf16[128,128]{1,0:T(8,128)(2,1)S(1)}, u32[]{:S(2)}, u32[]{:S(2)}) collective-permute-start(bf16[128,128]{1,0:T(8,128)(2,1)} %param.7), channel_id=1, source_target_pairs={{0,368},{1,369},{2,240},{3,241},{4,256},{5,257},{6,128},{7,129},{8... | collective-permute-start | bytes 98312 | tf_op jit(solution)/shard_map/ppermute | solution.py:177
  17.5 4.8 %collective-permute-done = bf16[128,128]{1,0:T(8,128)(2,1)S(1)} collective-permute-done((bf16[128,128]{1,0:T(8,128)(2,1)}, bf16[128,128]{1,0:T(8,128)(2,1)S(1)}, u32[]{:S(2)}, u32[]{:S(2)}) %collective-permute-start) | collective-permute-done | bytes 32800 | tf_op jit(solution)/shard_map/ppermute | solution.py:177
  22.3 14.1 %all_to_all.20 = bf16[4,128,128]{2,1,0:T(8,128)(2,1)S(1)} all-to-all(bf16[4,128,128]{2,1,0:T(8,128)(2,1)S(1)} %broadcast_in_dim.6), channel_id=1, replica_groups=mesh['x'=4,'step'=4,'side'=2,'z'=8,'core'=2] {'step'}, dimensions={0} | all-to-all | bytes 262144 | tf_op jit(solution)/shard_map/all_to_all | solution.py:167
  36.4 1.3 %broadcast_in_dim.7 = bf16[8,4,128,128]{3,2,1,0:T(8,128)(2,1)} broadcast(bf16[4,128,128]{2,1,0:T(8,128)(2,1)S(1)} %all_to_all.20), dimensions={1,2,3} | broadcast | bytes 1179648 | tf_op jit(solution)/shard_map/broadcast_in_dim | solution.py:181
  37.7 4.6 %all-to-all-start.1 = ((bf16[8,4,128,128]{3,2,1,0:T(8,128)(2,1)}), bf16[8,4,128,128]{3,2,1,0:T(8,128)(2,1)S(1)}, u32[]{:S(2)}, u32[]{:S(2)}) async-start(bf16[8,4,128,128]{3,2,1,0:T(8,128)(2,1)} %broadcast_in_dim.7), calls=%async_computation.1 | async-start | bytes 2097152 | tf_op jit(solution)/shard_map/all_to_all | solution.py:167
  42.3 0.0 reduce-scatter.2.cloned.1.call-start
  42.3 0.0 copy-done.10
  42.3 1.9 %collective-permute-start.1 = (bf16[896,256]{1,0:T(8,128)(2,1)S(1)}, bf16[896,256]{1,0:T(8,128)(2,1)S(1)}, u32[]{:S(2)}, u32[]{:S(2)}) collective-permute-start(bf16[896,256]{1,0:T(8,128)(2,1)S(1)} %copy-done.10), channel_id=1, source_target_pairs={{0,1},{1,0},{2,3},{3,2},{4,5},{5,4},{6,7},{7,6},{8,9},{9,8},{10,11... | collective-permute-start | bytes 1376264 | tf_op jit(solution)/shard_map/ppermute | solution.py:178
  44.3 1.8 %collective-permute-done.1.other_ref = bf16[896,256]{1,0:T(8,128)(2,1)S(1)} collective-permute-done((bf16[896,256]{1,0:T(8,128)(2,1)S(1)}, bf16[896,256]{1,0:T(8,128)(2,1)S(1)}, u32[]{:S(2)}, u32[]{:S(2)}) %collective-permute-start.1) | collective-permute-done | bytes 458784 | tf_op jit(solution)/shard_map/ppermute | solution.py:178
  46.1 9.7 %all-to-all-done.1.grad_ref = bf16[8,4,128,128]{3,2,1,0:T(8,128)(2,1)S(1)} async-done(((bf16[8,4,128,128]{3,2,1,0:T(8,128)(2,1)}), bf16[8,4,128,128]{3,2,1,0:T(8,128)(2,1)S(1)}, u32[]{:S(2)}, u32[]{:S(2)}) %all-to-all-start.1) | async-done | bytes 1048608 | tf_op jit(solution)/shard_map/all_to_all | solution.py:167
  55.7 0.0 copy-start.2
  55.7 2.6 %shard_map.76 = (bf16[8,128,896]{2,1,0:T(8,128)(2,1)}, f32[128,896]{1,0:T(8,128)S(1)}) custom-call(bf16[8,4,128,128]{3,2,1,0:T(8,128)(2,1)S(1)} %all-to-all-done.1.grad_ref, bf16[896,256]{1,0:T(8,128)(2,1)S(1)} %copy-done.10, bf16[896,256]{1,0:T(8,128)(2,1)S(1)} %collective-permute-done.1.other_ref), custom_call_target="tpu_custom_call" | custom-call | flops 939524096 | bytes 3670016 | tf_op jit(solution)/shard_map/pallas_call | solution.py:183
  58.3 0.0 copy-start.8
  58.3 0.8 copy-done.8
  59.1 0.0 reduce-scatter.2.cloned.1.call-update
  59.1 0.0 copy-done.2
  59.2 0.0 all-gather.2.cloned.1.call-done.hidden_ref
  59.2 0.0 copy-start
  59.2 1.5 %copy-done = bf16[1024,896]{1,0:T(8,128)(2,1)S(1)} copy-done((bf16[1024,896]{1,0:T(8,128)(2,1)S(1)}, bf16[1024,896]{1,0:T(8,128)(2,1)}, u32[]{:S(2)}) %copy-start) | copy-done | bytes 1835032
  60.7 2.3 %shard_map.77 = bf16[8,4,128,128]{3,2,1,0:T(8,128)(2,1)} custom-call(bf16[1024,896]{1,0:T(8,128)(2,1)S(1)} %copy-done, bf16[896,256]{1,0:T(8,128)(2,1)S(1)} %copy-done.10, bf16[896,256]{1,0:T(8,128)(2,1)S(1)} %collective-permute-done.1.other_ref), custom_call_target="tpu_custom_call" | custom-call | flops 939524096 | bytes 3670016 | tf_op jit(solution)/shard_map/pallas_call | solution.py:187
  63.0 0.0 copy-start.1
  63.0 5.2 %all-to-all-start.2 = ((bf16[8,4,128,128]{3,2,1,0:T(8,128)(2,1)}), bf16[8,4,128,128]{3,2,1,0:T(8,128)(2,1)S(1)}, u32[]{:S(2)}, u32[]{:S(2)}) async-start(bf16[8,4,128,128]{3,2,1,0:T(8,128)(2,1)} %shard_map.77), calls=%async_computation.2 | async-start | bytes 2097152 | tf_op jit(solution)/shard_map/all_to_all | solution.py:167
  68.2 0.0 copy-done.1
  68.2 0.0 copy-start.3
  68.2 1.2 %copy-done.3 = bf16[8,4,128,128]{3,2,1,0:T(8,128)(2,1)S(1)} copy-done((bf16[8,4,128,128]{3,2,1,0:T(8,128)(2,1)S(1)}, bf16[8,4,128,128]{3,2,1,0:T(8,128)(2,1)}, u32[]{:S(2)}) %copy-start.3) | copy-done | bytes 1048600
  69.4 2.2 %shard_map.81 = (f32[896,256]{1,0:T(8,128)S(1)}, f32[896,256]{1,0:T(8,128)}) custom-call(bf16[1024,896]{1,0:T(8,128)(2,1)S(1)} %copy-done.1, bf16[8,4,128,128]{3,2,1,0:T(8,128)(2,1)S(1)} %copy-done.3), custom_call_target="tpu_custom_call" | custom-call | flops 939524096 | bytes 3670016 | tf_op jit(solution)/shard_map/pallas_call | solution.py:203
  71.6 0.0 copy-start.4
  71.6 0.9 copy-done.4
  72.5 0.0 copy-start.5
  72.5 0.0 copy-start.6
  72.5 0.0 copy-start.7
  72.5 2.0 %collective-permute-start.3 = (f32[896,256]{1,0:T(8,128)}, f32[896,256]{1,0:T(8,128)S(1)}, u32[]{:S(2)}, u32[]{:S(2)}) collective-permute-start(f32[896,256]{1,0:T(8,128)} %get-tuple-element.27), channel_id=1, source_target_pairs={{0,1},{1,0},{2,3},{3,2},{4,5},{5,4},{6,7},{7,6},{8,9},{9,8},{10,11... | collective-permute-start | bytes 2752520 | tf_op jit(solution)/shard_map/ppermute | solution.py:207
  74.6 5.9 %all-to-all-done.2.parts_ref = bf16[8,4,128,128]{3,2,1,0:T(8,128)(2,1)S(1)} async-done(((bf16[8,4,128,128]{3,2,1,0:T(8,128)(2,1)}), bf16[8,4,128,128]{3,2,1,0:T(8,128)(2,1)S(1)}, u32[]{:S(2)}, u32[]{:S(2)}) %all-to-all-start.2) | async-done | bytes 1048608 | tf_op jit(solution)/shard_map/all_to_all | solution.py:167
  80.5 0.1 shard_map.78
  80.6 0.0 copy-start.9
  80.6 12.6 %all_to_all.21.parts_ref = bf16[4,128,128]{2,1,0:T(8,128)(2,1)S(1)} all-to-all(bf16[4,128,128]{2,1,0:T(8,128)(2,1)S(1)} %shard_map.78), channel_id=1, replica_groups=mesh['x'=4,'step'=4,'side'=2,'z'=8,'core'=2] {'step'}, dimensions={0} | all-to-all | bytes 262144 | tf_op jit(solution)/shard_map/all_to_all | solution.py:167
  93.3 7.3 %collective-permute-start.2 = (bf16[128,128]{1,0:T(8,128)(2,1)S(1)}, bf16[128,128]{1,0:T(8,128)(2,1)S(1)}, u32[]{:S(2)}, u32[]{:S(2)}) collective-permute-start(bf16[128,128]{1,0:T(8,128)(2,1)S(1)} %shard_map.79), channel_id=1, source_target_pairs={{368,0},{369,1},{240,2},{241,3},{256,4},{257,5},{128,6},{129,7},{0... | collective-permute-start | bytes 98312 | tf_op jit(solution)/shard_map/ppermute | solution.py:200
  100.6 0.0 collective-permute-done.3.b_ref
  100.6 0.0 copy-done.5
  100.6 0.8 shard_map.82
  101.4 4.0 %reduce-scatter.2.cloned.1.call-done.others_ref = bf16[128,896]{1,0:T(8,128)(2,1)} async-done(((bf16[1024,896]{1,0:T(8,128)(2,1)}), bf16[128,896]{1,0:T(8,128)(2,1)}) %reduce-scatter.2.cloned.1.call-update) | async-done | bytes 229392 | tf_op jit(solution)/shard_map/reduce_scatter | solution.py:191
  105.5 0.0 copy-done.6
  105.5 0.0 copy-done.7
  105.5 0.0 copy-done.9
  105.5 0.0 copy-start.11
  105.5 0.9 copy-done.11
  106.4 1.0 shard_map.80
  107.4 0.0 collective-permute-done.2
  107.4 0.6 copy.9
  (2 shorter events, 0.0 us)
Async XLA Ops:
  7.2 52.0 %all-gather.2.cloned.1.call-start = ((), (), s32[]{:S(2)}) async-start(), calls=%async_computation.5 | async-start | bytes 2064384 | tf_op jit(solution)/shard_map/all_gather | solution.py:175
  9.1 33.3 %copy-start.10 = (bf16[896,256]{1,0:T(8,128)(2,1)S(1)}, bf16[896,256]{1,0:T(8,128)(2,1)}, u32[]{:S(2)}) copy-start(bf16[896,256]{1,0:T(8,128)(2,1)} %own_ref.3) | copy-start | bytes 1376260
  9.1 13.2 %collective-permute-start = (bf16[128,128]{1,0:T(8,128)(2,1)}, bf16[128,128]{1,0:T(8,128)(2,1)S(1)}, u32[]{:S(2)}, u32[]{:S(2)}) collective-permute-start(bf16[128,128]{1,0:T(8,128)(2,1)} %param.7), channel_id=1, source_target_pairs={{0,368},{1,369},{2,240},{3,241},{4,256},{5,257},{6,128},{7,129},{8... | collective-permute-start | bytes 98312 | tf_op jit(solution)/shard_map/ppermute | solution.py:177
  37.7 18.1 %all-to-all-start.1 = ((bf16[8,4,128,128]{3,2,1,0:T(8,128)(2,1)}), bf16[8,4,128,128]{3,2,1,0:T(8,128)(2,1)S(1)}, u32[]{:S(2)}, u32[]{:S(2)}) async-start(bf16[8,4,128,128]{3,2,1,0:T(8,128)(2,1)} %broadcast_in_dim.7), calls=%async_computation.1 | async-start | bytes 2097152 | tf_op jit(solution)/shard_map/all_to_all | solution.py:167
  42.3 63.2 %reduce-scatter.2.cloned.1.call-start = ((), (), s32[]{:S(2)}) async-start(), calls=%async_computation.6 | async-start | bytes 2064384 | tf_op jit(solution)/shard_map/reduce_scatter | solution.py:191
  42.3 3.7 %collective-permute-start.1 = (bf16[896,256]{1,0:T(8,128)(2,1)S(1)}, bf16[896,256]{1,0:T(8,128)(2,1)S(1)}, u32[]{:S(2)}, u32[]{:S(2)}) collective-permute-start(bf16[896,256]{1,0:T(8,128)(2,1)S(1)} %copy-done.10), channel_id=1, source_target_pairs={{0,1},{1,0},{2,3},{3,2},{4,5},{5,4},{6,7},{7,6},{8,9},{9,8},{10,11... | collective-permute-start | bytes 1376264 | tf_op jit(solution)/shard_map/ppermute | solution.py:178
  55.7 3.4 %copy-start.2 = (bf16[8,4,128,128]{3,2,1,0:T(8,128)(2,1)}, bf16[8,4,128,128]{3,2,1,0:T(8,128)(2,1)S(1)}, u32[]{:S(2)}) copy-start(bf16[8,4,128,128]{3,2,1,0:T(8,128)(2,1)S(1)} %all-to-all-done.1.grad_ref) | copy-start | bytes 3145732
  58.3 0.8 copy-start.8
  59.2 1.5 %copy-start = (bf16[1024,896]{1,0:T(8,128)(2,1)S(1)}, bf16[1024,896]{1,0:T(8,128)(2,1)}, u32[]{:S(2)}) copy-start(bf16[1024,896]{1,0:T(8,128)(2,1)} %all-gather.2.cloned.1.call-done.hidden_ref) | copy-start | bytes 5505028
  63.0 5.2 %copy-start.1 = (bf16[1024,896]{1,0:T(8,128)(2,1)S(1)}, bf16[1024,896]{1,0:T(8,128)(2,1)}, u32[]{:S(2)}) copy-start(bf16[1024,896]{1,0:T(8,128)(2,1)} %all-gather.2.cloned.1.call-done.hidden_ref) | copy-start | bytes 5505028
  63.0 17.5 %all-to-all-start.2 = ((bf16[8,4,128,128]{3,2,1,0:T(8,128)(2,1)}), bf16[8,4,128,128]{3,2,1,0:T(8,128)(2,1)S(1)}, u32[]{:S(2)}, u32[]{:S(2)}) async-start(bf16[8,4,128,128]{3,2,1,0:T(8,128)(2,1)} %shard_map.77), calls=%async_computation.2 | async-start | bytes 2097152 | tf_op jit(solution)/shard_map/all_to_all | solution.py:167
  68.2 1.2 %copy-start.3 = (bf16[8,4,128,128]{3,2,1,0:T(8,128)(2,1)S(1)}, bf16[8,4,128,128]{3,2,1,0:T(8,128)(2,1)}, u32[]{:S(2)}) copy-start(bf16[8,4,128,128]{3,2,1,0:T(8,128)(2,1)} %copy-done.2) | copy-start | bytes 3145732
  71.6 0.9 copy-start.4
  72.5 28.1 %copy-start.5 = (f32[896,256]{1,0:T(8,128)S(1)}, f32[896,256]{1,0:T(8,128)}, u32[]{:S(2)}) copy-start(f32[896,256]{1,0:T(8,128)} %copy-done.4) | copy-start | bytes 2752516
  72.5 33.0 %copy-start.6 = (bf16[128,896]{1,0:T(8,128)(2,1)S(1)}, bf16[128,896]{1,0:T(8,128)(2,1)}, u32[]{:S(2)}) copy-start(bf16[128,896]{1,0:T(8,128)(2,1)} %gate_ref.3) | copy-start | bytes 688132
  72.5 33.0 %copy-start.7 = (bf16[128,896]{1,0:T(8,128)(2,1)S(1)}, bf16[128,896]{1,0:T(8,128)(2,1)}, u32[]{:S(2)}) copy-start(bf16[128,896]{1,0:T(8,128)(2,1)} %up_ref.3) | copy-start | bytes 688132
  72.5 28.1 %collective-permute-start.3 = (f32[896,256]{1,0:T(8,128)}, f32[896,256]{1,0:T(8,128)S(1)}, u32[]{:S(2)}, u32[]{:S(2)}) collective-permute-start(f32[896,256]{1,0:T(8,128)} %get-tuple-element.27), channel_id=1, source_target_pairs={{0,1},{1,0},{2,3},{3,2},{4,5},{5,4},{6,7},{7,6},{8,9},{9,8},{10,11... | collective-permute-start | bytes 2752520 | tf_op jit(solution)/shard_map/ppermute | solution.py:207
  80.6 24.9 %copy-start.9 = (f32[128,896]{1,0:T(8,128)S(1)}, f32[128,896]{1,0:T(8,128)}, u32[]{:S(2)}) copy-start(f32[128,896]{1,0:T(8,128)} %copy-done.8) | copy-start | bytes 1376260
  93.3 14.1 %collective-permute-start.2 = (bf16[128,128]{1,0:T(8,128)(2,1)S(1)}, bf16[128,128]{1,0:T(8,128)(2,1)S(1)}, u32[]{:S(2)}, u32[]{:S(2)}) collective-permute-start(bf16[128,128]{1,0:T(8,128)(2,1)S(1)} %shard_map.79), channel_id=1, source_target_pairs={{368,0},{369,1},{240,2},{241,3},{256,4},{257,5},{128,6},{129,7},{0... | collective-permute-start | bytes 98312 | tf_op jit(solution)/shard_map/ppermute | solution.py:200
  105.5 0.9 copy-start.11
Sparse Core Ops, SparseCore 0:
  10.7 48.3 all-gather.1
  61.9 43.4 reduce-scatter.1

commit v5 on v4

--- a/solution.py
+++ b/solution.py
@@ -100,17 +100,30 @@
         store.wait()
 
 
-def share_kernel(grad_ref, own_ref, other_ref, share_ref, mine_ref):
+def share_kernel(grad_ref, own_ref, other_ref, share_ref, mine_ref, share_out, sems):
     weights = jnp.concatenate([own_ref[...], other_ref[...]], axis=1)
-
-    def product(tokens):
-        grad = jnp.concatenate([grad_of(grad_ref, tokens, half) for half in range(2)], axis=1)
+    tokens = mine_ref.shape[0]
+    here = lax.axis_index("z")
+    parts, copies = 2, []
+    count = Z // parts
+
+    def product(blocks):
+        grad = jnp.concatenate([grad_of(grad_ref, blocks, half) for half in range(2)], axis=1)
         return lax.dot_general(grad, weights, (((1,), (1,)), ((), ())), preferred_element_type=jnp.float32)
 
-    share_ref[...] = product(range(Z)).astype(jnp.bfloat16).reshape(share_ref.shape)
-    here = lax.axis_index("z")
-    share_ref[here] = jnp.zeros(mine_ref.shape, jnp.bfloat16)
+    for i in range(parts):
+        z = pl.ds(i * count, count)
+        rows = product(range(i * count, (i + 1) * count))
+        share_out[z] = rows.astype(jnp.bfloat16).reshape(count, tokens, -1)
+
+        @pl.when(here // count == i)
+        def _():
+            share_out[here] = jnp.zeros(mine_ref.shape, jnp.bfloat16)
+
+        copies.append(started(share_out.at[z], share_ref.at[z], sems.at[i]))
     mine_ref[...] = product([here])
+    for copy in copies:
+        copy.wait()
 
 
 def output_kernel(hidden_ref, own_ref, other_ref, out_ref):
@@ -181,7 +194,12 @@
     grad = exchanged(jnp.broadcast_to(grad, (X * SIDES, steps, tokens, sub)), ("x", "side"))
 
     share, mine = kernel_call(
-        share_kernel, (shape((Z, tokens, units), bf16), shape(block, f32)), flops, 4 * rows * units
+        share_kernel,
+        (shape((Z, tokens, units), bf16), shape(block, f32)),
+        flops,
+        4 * rows * units,
+        out_specs=(pl.BlockSpec(memory_space=pl.ANY), pl.BlockSpec(memory_space=pltpu.VMEM)),
+        scratch_shapes=[vmem((Z, tokens, units), bf16), dma((2,))],
     )(grad, down_weight, other_weight)
     hidden_all, _ = together((hidden_all, mine))
     output = kernel_call(output_kernel, shape((X * SIDES, steps, tokens, sub), bf16), flops, 4 * rows * units)(

time: 115 us -> 115 us (level)
  the two profiles are of different devices: /device:TPU:16 before, /device:TPU:14 now
where the time goes in v5:
time: 115 us
  starting transfers between devices  33.1 us (29%)
  blocking collectives  28.5 us (25%)
  waiting for transfers between devices  21 us (18%)
  between operations  14.2 us (12%)
  Pallas kernels  10.8 us (9%)
  local copies, waits for them, and re-layouts  7.28 us (6%)
    all_to_all x2, blocking collectives, exchanged(): return lax.all_to_all(array, axis, split_axis=0, concat_axis=0, tiled=True)  28.5 us
    ppermute x1, starting transfers between devices, body(): grad = lax.ppermute(out_grad, AXES, there)  11.9 us
    all_to_all x2, starting transfers between devices, exchanged(): return lax.all_to_all(array, axis, split_axis=0, concat_axis=0, tiled=True)  11.2 us
    all_to_all x2, waiting for transfers between devices, exchanged(): return lax.all_to_all(array, axis, split_axis=0, concat_axis=0, tiled=True)  10.6 us
    unnamed x25, local copies, waits for them, and re-layouts  6.01 us
    ppermute x1, starting transfers between devices, body(): output = lax.ppermute(output, AXES, back)  5.96 us
    reduce_scatter x1, waiting for transfers between devices, body(): lax.psum_scatter(share.reshape(rows, units), 'z', scatter_dimension=0, ti...  5.67 us
    pallas_call x1, Pallas kernels, body(): kernel_call(share_kernel, (shape((Z, tokens, units), bf16), shape(block,...  2.55 us
  transfers between devices with their start and end apart: 8, of which 6 were waited for; matrix products, arithmetic and copies ran while one was open for 1% of the time, Pallas kernels for 8%

profile of v5, /device:TPU:14, one launch (start us, length us, event | category | flops | bytes accessed | tf_op | source)
XLA Modules:
  0.0 114.9 jit_solution(14408372304281687781)
XLA Ops:
  7.2 0.0 all-gather.2.cloned.1.call-start
  7.2 1.8 %shard_map.75 = bf16[128,896]{1,0:T(8,128)(2,1)} custom-call(bf16[128,896]{1,0:T(8,128)(2,1)} %gate_ref.3, bf16[128,896]{1,0:T(8,128)(2,1)} %up_ref.3), custom_call_target="tpu_custom_call" | custom-call | bytes 688128 | tf_op jit(solution)/shard_map/pallas_call | solution.py:63
  9.0 0.0 all-gather.2.cloned.1.call-update
  9.1 0.0 copy-start.10
  9.1 11.9 %collective-permute-start = (bf16[128,128]{1,0:T(8,128)(2,1)}, bf16[128,128]{1,0:T(8,128)(2,1)S(1)}, u32[]{:S(2)}, u32[]{:S(2)}) collective-permute-start(bf16[128,128]{1,0:T(8,128)(2,1)} %param.7), channel_id=1, source_target_pairs={{0,368},{1,369},{2,240},{3,241},{4,256},{5,257},{6,128},{7,129},{8... | collective-permute-start | bytes 98312 | tf_op jit(solution)/shard_map/ppermute | solution.py:190
  21.0 2.1 %collective-permute-done = bf16[128,128]{1,0:T(8,128)(2,1)S(1)} collective-permute-done((bf16[128,128]{1,0:T(8,128)(2,1)}, bf16[128,128]{1,0:T(8,128)(2,1)S(1)}, u32[]{:S(2)}, u32[]{:S(2)}) %collective-permute-start) | collective-permute-done | bytes 32800 | tf_op jit(solution)/shard_map/ppermute | solution.py:190
  23.1 14.6 %all_to_all.20 = bf16[4,128,128]{2,1,0:T(8,128)(2,1)S(1)} all-to-all(bf16[4,128,128]{2,1,0:T(8,128)(2,1)S(1)} %broadcast_in_dim.6), channel_id=1, replica_groups=mesh['x'=4,'step'=4,'side'=2,'z'=8,'core'=2] {'step'}, dimensions={0} | all-to-all | bytes 262144 | tf_op jit(solution)/shard_map/all_to_all | solution.py:180
  37.7 1.3 %broadcast_in_dim.7 = bf16[8,4,128,128]{3,2,1,0:T(8,128)(2,1)} broadcast(bf16[4,128,128]{2,1,0:T(8,128)(2,1)S(1)} %all_to_all.20), dimensions={1,2,3} | broadcast | bytes 1179648 | tf_op jit(solution)/shard_map/broadcast_in_dim | solution.py:194
  38.9 5.4 %all-to-all-start.1 = ((bf16[8,4,128,128]{3,2,1,0:T(8,128)(2,1)}), bf16[8,4,128,128]{3,2,1,0:T(8,128)(2,1)S(1)}, u32[]{:S(2)}, u32[]{:S(2)}) async-start(bf16[8,4,128,128]{3,2,1,0:T(8,128)(2,1)} %broadcast_in_dim.7), calls=%async_computation.1 | async-start | bytes 2097152 | tf_op jit(solution)/shard_map/all_to_all | solution.py:180
  44.3 0.0 reduce-scatter.2.cloned.1.call-start
  44.3 0.0 copy-done.10
  44.3 1.9 %collective-permute-start.1 = (bf16[896,256]{1,0:T(8,128)(2,1)S(1)}, bf16[896,256]{1,0:T(8,128)(2,1)S(1)}, u32[]{:S(2)}, u32[]{:S(2)}) collective-permute-start(bf16[896,256]{1,0:T(8,128)(2,1)S(1)} %copy-done.10), channel_id=1, source_target_pairs={{0,1},{1,0},{2,3},{3,2},{4,5},{5,4},{6,7},{7,6},{8,9},{9,8},{10,11... | collective-permute-start | bytes 1376264 | tf_op jit(solution)/shard_map/ppermute | solution.py:191
  46.3 1.8 %collective-permute-done.1.other_ref = bf16[896,256]{1,0:T(8,128)(2,1)S(1)} collective-permute-done((bf16[896,256]{1,0:T(8,128)(2,1)S(1)}, bf16[896,256]{1,0:T(8,128)(2,1)S(1)}, u32[]{:S(2)}, u32[]{:S(2)}) %collective-permute-start.1) | collective-permute-done | bytes 458784 | tf_op jit(solution)/shard_map/ppermute | solution.py:191
  48.0 6.9 %all-to-all-done.1.grad_ref = bf16[8,4,128,128]{3,2,1,0:T(8,128)(2,1)S(1)} async-done(((bf16[8,4,128,128]{3,2,1,0:T(8,128)(2,1)}), bf16[8,4,128,128]{3,2,1,0:T(8,128)(2,1)S(1)}, u32[]{:S(2)}, u32[]{:S(2)}) %all-to-all-start.1) | async-done | bytes 1048608 | tf_op jit(solution)/shard_map/all_to_all | solution.py:180
  54.9 0.0 copy-start.2
  54.9 2.6 %shard_map.76 = (bf16[8,128,896]{2,1,0:T(8,128)(2,1)}, f32[128,896]{1,0:T(8,128)S(1)}) custom-call(bf16[8,4,128,128]{3,2,1,0:T(8,128)(2,1)S(1)} %all-to-all-done.1.grad_ref, bf16[896,256]{1,0:T(8,128)(2,1)S(1)} %copy-done.10, bf16[896,256]{1,0:T(8,128)(2,1)S(1)} %collective-permute-done.1.other_ref), custom_call_target="tpu_custom_call" | custom-call | flops 939524096 | bytes 3670016 | tf_op jit(solution)/shard_map/pallas_call | solution.py:196
  57.5 0.0 copy-start.8
  57.5 0.8 copy-done.8
  58.3 0.0 reduce-scatter.2.cloned.1.call-update
  58.3 0.0 copy-done.2
  58.3 0.8 all-gather.2.cloned.1.call-done.hidden_ref
  59.1 0.0 copy-start
  59.1 1.5 %copy-done = bf16[1024,896]{1,0:T(8,128)(2,1)S(1)} copy-done((bf16[1024,896]{1,0:T(8,128)(2,1)S(1)}, bf16[1024,896]{1,0:T(8,128)(2,1)}, u32[]{:S(2)}) %copy-start) | copy-done | bytes 1835032
  60.6 2.3 %shard_map.77 = bf16[8,4,128,128]{3,2,1,0:T(8,128)(2,1)} custom-call(bf16[1024,896]{1,0:T(8,128)(2,1)S(1)} %copy-done, bf16[896,256]{1,0:T(8,128)(2,1)S(1)} %copy-done.10, bf16[896,256]{1,0:T(8,128)(2,1)S(1)} %collective-permute-done.1.other_ref), custom_call_target="tpu_custom_call" | custom-call | flops 939524096 | bytes 3670016 | tf_op jit(solution)/shard_map/pallas_call | solution.py:205
  62.9 0.0 copy-start.1
  62.9 5.8 %all-to-all-start.2 = ((bf16[8,4,128,128]{3,2,1,0:T(8,128)(2,1)}), bf16[8,4,128,128]{3,2,1,0:T(8,128)(2,1)S(1)}, u32[]{:S(2)}, u32[]{:S(2)}) async-start(bf16[8,4,128,128]{3,2,1,0:T(8,128)(2,1)} %shard_map.77), calls=%async_computation.2 | async-start | bytes 2097152 | tf_op jit(solution)/shard_map/all_to_all | solution.py:180
  68.7 0.0 copy-done.1
  68.7 0.0 copy-start.3
  68.7 1.2 %copy-done.3 = bf16[8,4,128,128]{3,2,1,0:T(8,128)(2,1)S(1)} copy-done((bf16[8,4,128,128]{3,2,1,0:T(8,128)(2,1)S(1)}, bf16[8,4,128,128]{3,2,1,0:T(8,128)(2,1)}, u32[]{:S(2)}) %copy-start.3) | copy-done | bytes 1048600
  70.0 2.2 %shard_map.81 = (f32[896,256]{1,0:T(8,128)S(1)}, f32[896,256]{1,0:T(8,128)}) custom-call(bf16[1024,896]{1,0:T(8,128)(2,1)S(1)} %copy-done.1, bf16[8,4,128,128]{3,2,1,0:T(8,128)(2,1)S(1)} %copy-done.3), custom_call_target="tpu_custom_call" | custom-call | flops 939524096 | bytes 3670016 | tf_op jit(solution)/shard_map/pallas_call | solution.py:221
  72.1 0.0 copy-start.4
  72.1 0.9 copy-done.4
  73.0 0.0 copy-start.5
  73.1 0.0 copy-start.6
  73.1 0.0 copy-start.7
  73.1 2.0 %collective-permute-start.3 = (f32[896,256]{1,0:T(8,128)}, f32[896,256]{1,0:T(8,128)S(1)}, u32[]{:S(2)}, u32[]{:S(2)}) collective-permute-start(f32[896,256]{1,0:T(8,128)} %get-tuple-element.27), channel_id=1, source_target_pairs={{0,1},{1,0},{2,3},{3,2},{4,5},{5,4},{6,7},{7,6},{8,9},{9,8},{10,11... | collective-permute-start | bytes 2752520 | tf_op jit(solution)/shard_map/ppermute | solution.py:225
  75.1 3.8 %all-to-all-done.2.parts_ref = bf16[8,4,128,128]{3,2,1,0:T(8,128)(2,1)S(1)} async-done(((bf16[8,4,128,128]{3,2,1,0:T(8,128)(2,1)}), bf16[8,4,128,128]{3,2,1,0:T(8,128)(2,1)S(1)}, u32[]{:S(2)}, u32[]{:S(2)}) %all-to-all-start.2) | async-done | bytes 1048608 | tf_op jit(solution)/shard_map/all_to_all | solution.py:180
  78.9 0.1 shard_map.78
  79.0 0.0 copy-start.9
  79.0 14.0 %all_to_all.21.parts_ref = bf16[4,128,128]{2,1,0:T(8,128)(2,1)S(1)} all-to-all(bf16[4,128,128]{2,1,0:T(8,128)(2,1)S(1)} %shard_map.78), channel_id=1, replica_groups=mesh['x'=4,'step'=4,'side'=2,'z'=8,'core'=2] {'step'}, dimensions={0} | all-to-all | bytes 262144 | tf_op jit(solution)/shard_map/all_to_all | solution.py:180
  93.0 6.0 %collective-permute-start.2 = (bf16[128,128]{1,0:T(8,128)(2,1)S(1)}, bf16[128,128]{1,0:T(8,128)(2,1)S(1)}, u32[]{:S(2)}, u32[]{:S(2)}) collective-permute-start(bf16[128,128]{1,0:T(8,128)(2,1)S(1)} %shard_map.79), channel_id=1, source_target_pairs={{368,0},{369,1},{240,2},{241,3},{256,4},{257,5},{128,6},{129,7},{0... | collective-permute-start | bytes 98312 | tf_op jit(solution)/shard_map/ppermute | solution.py:218
  99.0 0.0 collective-permute-done.3.b_ref
  99.0 0.0 copy-done.5
  99.0 0.8 shard_map.82
  99.8 5.7 %reduce-scatter.2.cloned.1.call-done.others_ref = bf16[128,896]{1,0:T(8,128)(2,1)} async-done(((bf16[1024,896]{1,0:T(8,128)(2,1)}), bf16[128,896]{1,0:T(8,128)(2,1)}) %reduce-scatter.2.cloned.1.call-update) | async-done | bytes 229392 | tf_op jit(solution)/shard_map/reduce_scatter | solution.py:209
  105.5 0.0 copy-done.6
  105.5 0.0 copy-done.7
  105.5 0.0 copy-done.9
  105.5 0.0 copy-start.11
  105.5 0.9 copy-done.11
  106.4 1.0 shard_map.80
  107.4 0.0 collective-permute-done.2
  107.4 0.6 copy.9
  (2 shorter events, 0.0 us)
Async XLA Ops:
  7.2 51.9 %all-gather.2.cloned.1.call-start = ((), (), s32[]{:S(2)}) async-start(), calls=%async_computation.5 | async-start | bytes 2064384 | tf_op jit(solution)/shard_map/all_gather | solution.py:188
  9.1 35.3 %copy-start.10 = (bf16[896,256]{1,0:T(8,128)(2,1)S(1)}, bf16[896,256]{1,0:T(8,128)(2,1)}, u32[]{:S(2)}) copy-start(bf16[896,256]{1,0:T(8,128)(2,1)} %own_ref.3) | copy-start | bytes 1376260
  9.1 14.0 %collective-permute-start = (bf16[128,128]{1,0:T(8,128)(2,1)}, bf16[128,128]{1,0:T(8,128)(2,1)S(1)}, u32[]{:S(2)}, u32[]{:S(2)}) collective-permute-start(bf16[128,128]{1,0:T(8,128)(2,1)} %param.7), channel_id=1, source_target_pairs={{0,368},{1,369},{2,240},{3,241},{4,256},{5,257},{6,128},{7,129},{8... | collective-permute-start | bytes 98312 | tf_op jit(solution)/shard_map/ppermute | solution.py:190
  38.9 16.0 %all-to-all-start.1 = ((bf16[8,4,128,128]{3,2,1,0:T(8,128)(2,1)}), bf16[8,4,128,128]{3,2,1,0:T(8,128)(2,1)S(1)}, u32[]{:S(2)}, u32[]{:S(2)}) async-start(bf16[8,4,128,128]{3,2,1,0:T(8,128)(2,1)} %broadcast_in_dim.7), calls=%async_computation.1 | async-start | bytes 2097152 | tf_op jit(solution)/shard_map/all_to_all | solution.py:180
  44.3 61.2 %reduce-scatter.2.cloned.1.call-start = ((), (), s32[]{:S(2)}) async-start(), calls=%async_computation.6 | async-start | bytes 2064384 | tf_op jit(solution)/shard_map/reduce_scatter | solution.py:209
  44.3 3.7 %collective-permute-start.1 = (bf16[896,256]{1,0:T(8,128)(2,1)S(1)}, bf16[896,256]{1,0:T(8,128)(2,1)S(1)}, u32[]{:S(2)}, u32[]{:S(2)}) collective-permute-start(bf16[896,256]{1,0:T(8,128)(2,1)S(1)} %copy-done.10), channel_id=1, source_target_pairs={{0,1},{1,0},{2,3},{3,2},{4,5},{5,4},{6,7},{7,6},{8,9},{9,8},{10,11... | collective-permute-start | bytes 1376264 | tf_op jit(solution)/shard_map/ppermute | solution.py:191
  54.9 3.4 %copy-start.2 = (bf16[8,4,128,128]{3,2,1,0:T(8,128)(2,1)}, bf16[8,4,128,128]{3,2,1,0:T(8,128)(2,1)S(1)}, u32[]{:S(2)}) copy-start(bf16[8,4,128,128]{3,2,1,0:T(8,128)(2,1)S(1)} %all-to-all-done.1.grad_ref) | copy-start | bytes 3145732
  57.5 0.8 copy-start.8
  59.1 1.5 %copy-start = (bf16[1024,896]{1,0:T(8,128)(2,1)S(1)}, bf16[1024,896]{1,0:T(8,128)(2,1)}, u32[]{:S(2)}) copy-start(bf16[1024,896]{1,0:T(8,128)(2,1)} %all-gather.2.cloned.1.call-done.hidden_ref) | copy-start | bytes 5505028
  62.9 5.8 %copy-start.1 = (bf16[1024,896]{1,0:T(8,128)(2,1)S(1)}, bf16[1024,896]{1,0:T(8,128)(2,1)}, u32[]{:S(2)}) copy-start(bf16[1024,896]{1,0:T(8,128)(2,1)} %all-gather.2.cloned.1.call-done.hidden_ref) | copy-start | bytes 5505028
  62.9 16.0 %all-to-all-start.2 = ((bf16[8,4,128,128]{3,2,1,0:T(8,128)(2,1)}), bf16[8,4,128,128]{3,2,1,0:T(8,128)(2,1)S(1)}, u32[]{:S(2)}, u32[]{:S(2)}) async-start(bf16[8,4,128,128]{3,2,1,0:T(8,128)(2,1)} %shard_map.77), calls=%async_computation.2 | async-start | bytes 2097152 | tf_op jit(solution)/shard_map/all_to_all | solution.py:180
  68.7 1.2 %copy-start.3 = (bf16[8,4,128,128]{3,2,1,0:T(8,128)(2,1)S(1)}, bf16[8,4,128,128]{3,2,1,0:T(8,128)(2,1)}, u32[]{:S(2)}) copy-start(bf16[8,4,128,128]{3,2,1,0:T(8,128)(2,1)} %copy-done.2) | copy-start | bytes 3145732
  72.1 0.9 copy-start.4
  73.0 25.9 %copy-start.5 = (f32[896,256]{1,0:T(8,128)S(1)}, f32[896,256]{1,0:T(8,128)}, u32[]{:S(2)}) copy-start(f32[896,256]{1,0:T(8,128)} %copy-done.4) | copy-start | bytes 2752516
  73.1 32.5 %copy-start.6 = (bf16[128,896]{1,0:T(8,128)(2,1)S(1)}, bf16[128,896]{1,0:T(8,128)(2,1)}, u32[]{:S(2)}) copy-start(bf16[128,896]{1,0:T(8,128)(2,1)} %gate_ref.3) | copy-start | bytes 688132
  73.1 32.5 %copy-start.7 = (bf16[128,896]{1,0:T(8,128)(2,1)S(1)}, bf16[128,896]{1,0:T(8,128)(2,1)}, u32[]{:S(2)}) copy-start(bf16[128,896]{1,0:T(8,128)(2,1)} %up_ref.3) | copy-start | bytes 688132
  73.1 25.9 %collective-permute-start.3 = (f32[896,256]{1,0:T(8,128)}, f32[896,256]{1,0:T(8,128)S(1)}, u32[]{:S(2)}, u32[]{:S(2)}) collective-permute-start(f32[896,256]{1,0:T(8,128)} %get-tuple-element.27), channel_id=1, source_target_pairs={{0,1},{1,0},{2,3},{3,2},{4,5},{5,4},{6,7},{7,6},{8,9},{9,8},{10,11... | collective-permute-start | bytes 2752520 | tf_op jit(solution)/shard_map/ppermute | solution.py:225
  79.0 26.5 %copy-start.9 = (f32[128,896]{1,0:T(8,128)S(1)}, f32[128,896]{1,0:T(8,128)}, u32[]{:S(2)}) copy-start(f32[128,896]{1,0:T(8,128)} %copy-done.8) | copy-start | bytes 1376260
  93.0 14.4 %collective-permute-start.2 = (bf16[128,128]{1,0:T(8,128)(2,1)S(1)}, bf16[128,128]{1,0:T(8,128)(2,1)S(1)}, u32[]{:S(2)}, u32[]{:S(2)}) collective-permute-start(bf16[128,128]{1,0:T(8,128)(2,1)S(1)} %shard_map.79), channel_id=1, source_target_pairs={{368,0},{369,1},{240,2},{241,3},{256,4},{257,5},{128,6},{129,7},{0... | collective-permute-start | bytes 98312 | tf_op jit(solution)/shard_map/ppermute | solution.py:218
  105.5 0.9 copy-start.11
Sparse Core Ops, SparseCore 0:
  10.7 48.4 all-gather.1
  62.0 43.4 reduce-scatter.1
